TPU v7x, 32 devices: a whole 2x2x4 slice. The times are simulated.
32 devices in a mesh: ens: 2 (over y), region: 4 (over z), bin: 2 (over x), pt: 2 (over core).
Axes of the slice: x: 2, y: 2, z: 4, core: 2. Of those that a mesh axis runs over, the one named last changes fastest.
Arguments:
- spectrum: float32 [864, 64, 512], P('ens', ('region', 'bin'), 'pt'), parts along dimension 0, may hold values from 0.1 to 2
- wind_u: float32 [128, 512], P(('ens', 'region', 'bin'), 'pt'), parts along dimension 0, may hold values from -5 to 5
- wind_v: float32 [128, 512], P(('ens', 'region', 'bin'), 'pt'), parts along dimension 0, may hold values from -5 to 5
- sea_mask: int32 [64, 512], P('region', 'pt'), may hold values from 0 to 1, as said below
- depth_factor: float32 [64, 512], P('region', 'pt'), may hold values from 0.4 to 1
- slope_x: float32 [64, 512], P('region', 'pt'), may hold values from -0.5 to 0.5
- slope_y: float32 [64, 512], P('region', 'pt'), may hold values from -0.5 to 0.5
Outputs:
- updated: float32 [864, 64, 512], P('ens', ('region', 'bin'), 'pt'), parts along dimension 0
There are 2 independent parts, one for each index of `ens`. A program takes and returns all parts, laid end to end along the dimension named above; an argument that names none is the same for every part. Nothing has to cross between parts.
Inputs may be any that keep to these rules, and one draw needn't show every extreme that they name: `sea_mask`: the grid's first and last rows are land.
All inputs are finite; a program needn't handle non-finite values.
Results may differ from a plain program's by a relative error of at most 0.00002.
Values sent between devices are 32-bit elements; how exact they have to be, the bound alone decides.
No kernel may reach another device: no remote copies, remote signals or barrier semaphores. Data moves between devices by JAX's collectives and lax.ppermute only.
A program may use at most 128 MiB of HBM per device.

v0:
```python
import math

import jax
import jax.numpy as jnp
import numpy as np
from jax import lax
from jax.experimental import pallas as pl
from jax.experimental.pallas import tpu as pltpu
from jax.sharding import PartitionSpec as P

F = 12
DIRS = 36
SUB = 4
ROWS = 8
LANES = 128
TILES = 2
HALF = DIRS // 2
SENT = [HALF - 1 + 2 * (SUB - k) for k in range(1, SUB + 1)]
PACK = sum(SENT)
GEO = 16
CHUNKS = (6, 4, 2)
STRIP = 2 * SUB + 2
EDGES = DIRS + 3
EDGE_ROWS = 96
PITCH = ROWS + 2 * SUB
PAD = 8
HEIGHT = DIRS * PITCH + 2 * PAD
SPAN = DIRS * ROWS

SIGMA = 0.6 * 1.1 ** np.arange(F, dtype=np.float64)
WEIGHT = SIGMA / (DIRS * SIGMA.sum())


def quarter_exact(fn):
    values = np.array([fn(2.0 * math.pi * d / DIRS) for d in range(DIRS)])
    values[np.abs(values) < 1e-9] = 0.0
    return [float(x) for x in values]


COS = quarter_exact(math.cos)
SIN = quarter_exact(math.sin)
SPEED = 0.27 / SIGMA


def of_freq(values, f):
    if isinstance(f, int):
        return float(values[f])
    out = jnp.float32(values[0])
    for i in range(1, F):
        out = jnp.where(f == i, jnp.float32(values[i]), out)
    return out


HBM = pl.BlockSpec(memory_space=pltpu.HBM)
VMEM = pl.BlockSpec(memory_space=pltpu.VMEM)
ANY = pl.BlockSpec(memory_space=pl.ANY)


def segments(up):
    out, row = [], 0
    for k in range(1, SUB + 1):
        low = 1 - (SUB - k) + (0 if up else HALF)
        left, at = SENT[k - 1], low
        while left > 0:
            first = at % DIRS
            count = min(left, DIRS - first)
            out.append((k, first, count, row))
            row, at, left = row + count, at + count, left - count
    return out


def lane_iota():
    return lax.broadcasted_iota(jnp.int32, (ROWS, LANES), 1)


def own_lanes():
    own = jnp.zeros((ROWS, LANES), jnp.bool_)
    for f in range(F):
        own = own | (lane_iota() == f * STRIP + SUB) | (lane_iota() == f * STRIP + SUB + 1)
    return own


def put_edges(pairs):
    lanes = lane_iota()
    packed = jnp.zeros((ROWS, LANES), jnp.float32)
    for f, (first_tile, last_tile) in enumerate(pairs):
        ends = jnp.where(lanes < LANES // 2, first_tile, last_tile)
        at = f * STRIP
        packed = jnp.where(lanes >= at, pltpu.roll(ends, (at + SUB) % LANES, 1), packed)
        packed = jnp.where(lanes >= at + SUB + 1, pltpu.roll(ends, (at + SUB + 2) % LANES, 1), packed)
    return packed


def split(value):
    return value[:, :LANES], value[:, LANES:]


def make_sources(raw, src, push, inverse, f, base):
    sig = of_freq(SIGMA, f)
    for t in range(TILES):
        for d in range(DIRS):
            grown = raw[t, f * DIRS + d] * (1.0 + sig * push[t, d])
            row = base + d * ROWS
            src[t, pl.ds(row, ROWS), :] = grown * inverse[t]


def make_packs(src, base, local, line, up_ref, down_ref):
    for ref, up in ((up_ref, True), (down_ref, False)):
        for k, d0, count, row in segments(up):
            j = ROWS - k if up else k - 1
            for t in range(TILES):
                line[t, row : row + count, :] = src[t, pl.ds(base + d0 * ROWS + j, count, stride=ROWS), :]
        for m in range(PACK // ROWS):
            rows = pl.ds(pl.multiple_of(local * PACK + m * ROWS, ROWS), ROWS)
            for t in range(TILES):
                ref[rows, t * LANES : (t + 1) * LANES] = line[t, m * ROWS : (m + 1) * ROWS, :]


def head_kernel(
    spec, u_hbm, v_hbm, mask_hbm, depth_hbm, sx_hbm, sy_hbm,
    raw, src0, push, damp_ref, geo, up_ref, down_ref,
    u_ref, v_ref, mask_ref, depth_ref, sx_ref, sy_ref, line, small_sem, in_sem,
):
    off = pl.multiple_of(lax.axis_index("bin") * ROWS, ROWS)
    own = pl.ds(off, ROWS)
    small = [
        pltpu.make_async_copy(a, b, small_sem.at[i])
        for i, (a, b) in enumerate(
            (
                (u_hbm, u_ref),
                (v_hbm, v_ref),
                (mask_hbm.at[own], mask_ref),
                (depth_hbm.at[own], depth_ref),
                (sx_hbm.at[own], sx_ref),
                (sy_hbm.at[own], sy_ref),
            )
        )
    ]

    def load(f, t):
        return pltpu.make_async_copy(
            spec.at[pl.ds(f * DIRS, DIRS), :, pl.ds(t * LANES, LANES)],
            raw.at[t, pl.ds(f * DIRS, DIRS)],
            in_sem.at[f, t],
        )

    for copy in small:
        copy.start()
    for f in range(F):
        for t in range(TILES):
            load(f, t).start()
    for copy in small:
        copy.wait()

    mask = mask_ref[...].astype(jnp.float32)
    fields = (depth_ref[...] * mask, sx_ref[...] * mask, sy_ref[...] * mask)
    tail = CHUNKS[0] * PACK
    for g in range(3):
        for t, tile in enumerate(split(fields[g])):
            geo[g, t] = tile
        rows = slice(tail + g * SUB, tail + (g + 1) * SUB)
        up_ref[rows, :] = fields[g][ROWS - SUB :, :]
        down_ref[rows, :] = fields[g][:SUB, :]
    for ref in (up_ref, down_ref):
        ref[tail + 3 * SUB : tail + GEO, :] = jnp.zeros((GEO - 3 * SUB, TILES * LANES), jnp.float32)
    for t, tile in enumerate(split(mask)):
        geo[3, t] = tile
    u, v = split(u_ref[...]), split(v_ref[...])
    for d in range(DIRS):
        for t in range(TILES):
            lean = jnp.maximum(u[t] * COS[d] + v[t] * SIN[d], 0.0)
            push[t, d] = 0.5 * lean * lean

    zero = jnp.zeros((ROWS, LANES), jnp.float32)
    sums = [(zero, zero)] * TILES
    for f in range(F):
        for t in range(TILES):
            load(f, t).wait()
            parts = [raw[t, f * DIRS + d] for d in range(4)]
            for d in range(4, DIRS):
                parts[d % 4] = parts[d % 4] + raw[t, f * DIRS + d]
            total = (parts[0] + parts[1]) + (parts[2] + parts[3])
            energy, first = sums[t]
            sums[t] = energy + float(WEIGHT[f]) * total, first + float(WEIGHT[f] * SIGMA[f]) * total
    damps = []
    for t, (energy, first) in enumerate(sums):
        mean_sigma = first / energy
        steep = energy * mean_sigma * mean_sigma / 1.5
        damps.append(0.5 * steep * steep / mean_sigma)
        damp_ref[t] = damps[t]

    def body(f, carry):
        inverse = [geo[3, t] / (1.0 + of_freq(SIGMA, f) * damps[t]) for t in range(TILES)]
        base = pl.multiple_of(f * SPAN, SPAN)
        make_sources(raw, src0, push, inverse, f, base)
        make_packs(src0, base, f, line, up_ref, down_ref)
        return carry

    lax.fori_loop(0, CHUNKS[0], body, 0)


def rest_kernel(raw, src0, push, damp, geo, *refs):
    n = len(CHUNKS) - 1
    src, edge = refs[:2]
    ups, downs, line = refs[2 : 2 + n], refs[2 + n : 2 + 2 * n], refs[2 + 2 * n]
    at = CHUNKS[0]
    for c in range(n):
        def body(local, carry, c=c, at=at):
            f = at + local
            inverse = [geo[3, t] / (1.0 + of_freq(SIGMA, f) * damp[t]) for t in range(TILES)]
            base = pl.multiple_of((f - CHUNKS[0]) * SPAN, SPAN)
            make_sources(raw, src, push, inverse, f, base)
            make_packs(src, base, local, line, ups[c], downs[c])
            return carry

        lax.fori_loop(0, CHUNKS[c + 1], body, 0)
        at += CHUNKS[c + 1]

    def edges(d, carry):
        pairs = []
        for f in range(F):
            ref, local = (src0, f) if f < CHUNKS[0] else (src, f - CHUNKS[0])
            row = pl.ds(pl.multiple_of(local * SPAN + d * ROWS, ROWS), ROWS)
            pairs.append((ref[0, row, :], ref[1, row, :]))
        edge[pl.ds(pl.multiple_of(d * ROWS, ROWS), ROWS), :] = put_edges(pairs)
        return carry

    lax.fori_loop(0, DIRS, edges, 0, unroll=4)
    for g in range(3):
        edge[(DIRS + g) * ROWS : (DIRS + g + 1) * ROWS, :] = put_edges([(geo[g, 0], geo[g, 1])] * F)


def join_kernel(own, other, edge, up_ref, down_ref):
    lanes = own_lanes()
    for d in range(EDGES):
        rows = slice(d * ROWS, (d + 1) * ROWS)
        edge[rows, :] = jnp.where(lanes, own[rows, :], other[rows, :])
    for ref, up in ((up_ref, True), (down_ref, False)):
        for k, d0, count, row in segments(up):
            j = ROWS - k if up else k - 1
            ref[row : row + count, :] = edge[pl.ds(d0 * ROWS + j, count, stride=ROWS), :]
        for g in range(3):
            first = (DIRS + g) * ROWS + (ROWS - SUB if up else 0)
            ref[PACK + g * SUB : PACK + (g + 1) * SUB, :] = edge[first : first + SUB, :]
        ref[PACK + 3 * SUB :, :] = jnp.zeros((EDGE_ROWS - PACK - 3 * SUB, LANES), jnp.float32)


def border_kernel(own, up, down, field):
    zero = jnp.zeros((ROWS, LANES), jnp.float32)
    for s in range(SUB):
        field[s, :PAD, :] = zero
        field[s, HEIGHT - PAD :, :] = zero
    for d in range(DIRS + 1):
        row = PAD + d * PITCH - SUB
        field[0, row : row + 2 * SUB, :] = zero
    for d in range(DIRS):
        row = PAD + d * PITCH + SUB
        field[0, row : row + ROWS, :] = own[d * ROWS : (d + 1) * ROWS, :]
    halves = (up[...], down[...])
    for value, is_up in zip(halves, (True, False)):
        for k, d0, count, row in segments(is_up):
            place = PAD + d0 * PITCH + (SUB - k if is_up else SUB + ROWS + k - 1)
            field[0, pl.ds(place, count, stride=PITCH), :] = value[row : row + count]
    speed = jnp.zeros((ROWS, LANES), jnp.float32)
    for f in range(F):
        speed = jnp.where(lane_iota() >= f * STRIP, float(SPEED[f]), speed)
    coefficients = []
    for half in range(2):
        geo = []
        for g in range(3):
            mine = own[(DIRS + g) * ROWS + half * SUB : (DIRS + g) * ROWS + (half + 1) * SUB, :]
            halo = halves[half][PACK + g * SUB : PACK + (g + 1) * SUB]
            geo.append(speed * jnp.concatenate([mine, halo] if half else [halo, mine], axis=0))
        coefficients.append((geo[0], 0.5 * geo[1], 0.5 * geo[2]))
    for step in range(SUB - 1):
        for half in range(2):
            depth, sx, sy = coefficients[half]

            def load(d, shift=0):
                row = PAD + (d % DIRS) * PITCH + half * ROWS + shift
                return field[step, row : row + ROWS, :]

            for d in range(DIRS):
                west, south = COS[d] >= 0.0, SIN[d] >= 0.0
                cos, sin = abs(COS[d]), abs(SIN[d])
                now = load(d)
                up_x = pltpu.roll(now, 1 if west else LANES - 1, 1)
                up_y = load(d, -1 if south else 1)
                vt = SIN[d] * sx - COS[d] * sy
                up_t = jnp.where(vt > 0.0, load(d - 1), load(d + 1))
                moved = depth * (cos * up_x + sin * up_y - (cos + sin) * now) + jnp.abs(vt) * (up_t - now)
                row = PAD + d * PITCH + half * ROWS
                field[step + 1, row : row + ROWS, :] = now + moved


def step_kernel(first, start, *refs):
    if first:
        (src, up, down, border, geo_own, geo_up, geo_down, out, geo, field_a, field_b, turn) = refs
    else:
        (src, up, down, border, geo, _, out, token, field_a, field_b, turn) = refs
        token[...] = jnp.zeros((ROWS, LANES), jnp.float32)

    @pl.when(pl.program_id(0) == 0)
    def _():
        if first:
            for g in range(3):
                rows = slice(g * SUB, (g + 1) * SUB)
                for t in range(TILES):
                    lanes = slice(t * LANES, (t + 1) * LANES)
                    geo[g, t, :SUB] = geo_up[rows, lanes]
                    geo[g, t, SUB : SUB + ROWS] = geo_own[g, t]
                    geo[g, t, SUB + ROWS :] = geo_down[rows, lanes]
        zero = jnp.zeros((ROWS, LANES), jnp.float32)
        for t in range(TILES):
            for field in (field_a, field_b):
                field[t, :PAD, :] = zero
                field[t, HEIGHT - PAD :, :] = zero
            for d in range(DIRS + 1):
                row = PAD + d * PITCH - SUB
                field_a[t, row : row + 2 * SUB, :] = zero
        for t in range(TILES):
            for half in range(2):
                rows = slice(half * ROWS, (half + 1) * ROWS)
                sx, sy = 0.5 * geo[1, t, rows], 0.5 * geo[2, t, rows]
                for d in range(DIRS):
                    turn[t, d * PITCH + half * ROWS : d * PITCH + (half + 1) * ROWS, :] = SIN[d] * sx - COS[d] * sy

    for d in range(DIRS):
        row = PAD + d * PITCH + SUB
        for t in range(TILES):
            field_a[t, row : row + ROWS, :] = src[t, d * ROWS : (d + 1) * ROWS, :]
    for ref, is_up in ((up, True), (down, False)):
        for k, d0, count, row in segments(is_up):
            place = PAD + d0 * PITCH + (SUB - k if is_up else SUB + ROWS + k - 1)
            place = pl.ds(place, count, stride=PITCH)
            for t in range(TILES):
                field_a[t, place, :] = ref[row : row + count, t * LANES : (t + 1) * LANES]

    freq = start + pl.program_id(0)
    speed = of_freq(SPEED, freq)
    lanes = lane_iota()
    at_first, at_last = lanes == 0, lanes == LANES - 1
    to_first = LANES - (freq * STRIP + SUB - 1)
    to_last = LANES - 1 - (freq * STRIP + SUB + 2)

    def advance(step, old, new):
        last = step == SUB - 1
        for part in (SUB,) if last else (0, ROWS):
            depth = [speed * geo[0, t, part : part + ROWS] for t in range(TILES)]

            def load(d, shift=0):
                row = PAD + (d % DIRS) * PITCH + part + shift
                return [old[t, row : row + ROWS, :] for t in range(TILES)]

            before, now = load(-1), load(0)
            initial = now
            for d in range(DIRS):
                after = load(d + 1) if d < DIRS - 1 else initial
                west, south = COS[d] >= 0.0, SIN[d] >= 0.0
                cos, sin = abs(COS[d]), abs(SIN[d])
                row = PAD + d * PITCH + part
                outer = pltpu.roll(border[step, row : row + ROWS, :], to_first if west else to_last, 1)
                rolled = [pltpu.roll(x, 1 if west else LANES - 1, 1) for x in now]
                up_y = load(d, -1 if south else 1)
                for t in range(TILES):
                    if west:
                        up_x = jnp.where(at_first, rolled[t - 1] if t else outer, rolled[t])
                    else:
                        up_x = jnp.where(at_last, rolled[t + 1] if t < TILES - 1 else outer, rolled[t])
                    vt = turn[t, d * PITCH + part : d * PITCH + part + ROWS, :]
                    up_t = jnp.where(vt > 0.0, before[t], after[t])
                    moved = depth[t] * (cos * up_x + sin * up_y[t] - (cos + sin) * now[t])
                    value = now[t] + (moved + speed * jnp.abs(vt) * (up_t - now[t]))
                    if last:
                        out[d, :, t * LANES : (t + 1) * LANES] = value
                    else:
                        new[t, row : row + ROWS, :] = value
                before, now = now, after

    fields = (field_a, field_b)
    for step in range(SUB):
        advance(step, fields[step % 2], fields[(step + 1) % 2])


def after(value, *others):
    return lax.optimization_barrier((value, *others))[0]


def per_device(spectrum, wind_u, wind_v, sea_mask, depth_factor, slope_x, slope_y):
    nbins, rows, cols = spectrum.shape
    assert (nbins, rows, cols) == (F * DIRS, ROWS, TILES * LANES)
    assert lax.axis_size("pt") == 2
    f32 = jnp.float32
    shape = lambda *s: jax.ShapeDtypeStruct(s, f32)
    scratch = lambda *s: pltpu.VMEM(s, f32)
    heights = [c * PACK + (GEO if i == 0 else 0) for i, c in enumerate(CHUNKS)]
    params = pltpu.CompilerParams(vmem_limit_bytes=32 * 2**20)
    cost = pl.CostEstimate(flops=1000, bytes_accessed=1000, transcendentals=0)
    tile = (rows, LANES)

    pinned = [
        pltpu.with_memory_space_constraint(x, pltpu.HBM)
        for x in (spectrum, wind_u, wind_v, sea_mask, depth_factor, slope_x, slope_y)
    ]
    raw, src0, push, damp, geo_own, up0, down0 = pl.pallas_call(
        head_kernel,
        out_shape=[
            shape(TILES, nbins, *tile),
            shape(TILES, CHUNKS[0] * SPAN, LANES),
            shape(TILES, DIRS, *tile),
            shape(TILES, *tile),
            shape(4, TILES, *tile),
            shape(heights[0], cols),
            shape(heights[0], cols),
        ],
        in_specs=[HBM] * 7,
        out_specs=[VMEM] * 7,
        scratch_shapes=[pltpu.VMEM((rows, cols), x.dtype) for x in (wind_u, wind_v, sea_mask, depth_factor, slope_x, slope_y)]
        + [scratch(TILES, PACK, LANES), pltpu.SemaphoreType.DMA((6,)), pltpu.SemaphoreType.DMA((F, TILES))],
        compiler_params=params,
        cost_estimate=cost,
        name="head",
    )(*pinned)

    n = len(CHUNKS) - 1
    outs = pl.pallas_call(
        rest_kernel,
        out_shape=[
            shape(TILES, (F - CHUNKS[0]) * SPAN, LANES),
            shape(EDGES * rows, LANES),
            *[shape(h, cols) for h in heights[1:]] * 2,
        ],
        in_specs=[VMEM] * 5,
        out_specs=[VMEM] * (2 + 2 * n),
        scratch_shapes=[scratch(TILES, PACK, LANES)],
        compiler_params=params,
        cost_estimate=cost,
        name="rest",
    )(raw, src0, push, damp, geo_own)
    src, edge = outs[:2]
    ups, downs = [up0, *outs[2 : 2 + n]], [down0, *outs[2 + n :]]

    blocks = lax.axis_size("region") * lax.axis_size("bin")
    up_pairs = [(i, i + 1) for i in range(blocks - 1)]
    down_pairs = [(j, i) for i, j in up_pairs]
    send_up = lambda x: lax.ppermute(x, ("region", "bin"), up_pairs)
    send_down = lambda x: lax.ppermute(x, ("region", "bin"), down_pairs)

    from_south, from_north = [send_up(ups[0])], [send_down(downs[0])]
    other = lax.ppermute(edge, "pt", [(0, 1), (1, 0)])
    edge, edge_up, edge_down = pl.pallas_call(
        join_kernel,
        out_shape=[shape(EDGES * rows, LANES), shape(EDGE_ROWS, LANES), shape(EDGE_ROWS, LANES)],
        in_specs=[VMEM] * 2,
        out_specs=[VMEM] * 3,
        compiler_params=params,
        cost_estimate=cost,
        name="join",
    )(edge, other)
    edge_south, edge_north = send_up(edge_up), send_down(edge_down)
    border = pl.pallas_call(
        border_kernel,
        out_shape=shape(SUB, HEIGHT, LANES),
        in_specs=[VMEM] * 3,
        out_specs=VMEM,
        compiler_params=params,
        cost_estimate=cost,
        name="border",
    )(edge, edge_south, edge_north)
    token = (edge_south, edge_north)

    block = pl.BlockSpec
    start, geo, result = 0, None, None
    for c, count in enumerate(CHUNKS):
        first = c == 0
        at = start
        if c + 1 < n + 1:
            from_south.append(send_up(after(ups[c + 1], *token)))
            from_north.append(send_down(after(downs[c + 1], *token)))
        source_at = at - (0 if first else CHUNKS[0])
        operands = [src0 if first else src, from_south[c], from_north[c], border]
        in_specs = [
            block((TILES, SPAN, LANES), lambda i, at=source_at: (0, at + i, 0)),
            block((PACK, cols), lambda i: (i, 0)),
            block((PACK, cols), lambda i: (i, 0)),
            block((SUB, HEIGHT, LANES), lambda i: (0, 0, 0)),
        ]
        geo_shape = (3, TILES, PITCH, LANES)
        geo_block = block(geo_shape, lambda i: (0, 0, 0, 0))
        out_shape = [shape(nbins, rows, cols)]
        out_specs = [block((DIRS, rows, cols), lambda i, at=at: (at + i, 0, 0))]
        aliases = {}
        if first:
            row = count * PACK // GEO
            operands += [geo_own, from_south[c], from_north[c]]
            in_specs += [
                block((4, TILES, *tile), lambda i: (0, 0, 0, 0)),
                block((GEO, cols), lambda i, g=row: (g, 0)),
                block((GEO, cols), lambda i, g=row: (g, 0)),
            ]
            out_shape.append(shape(*geo_shape))
            out_specs.append(geo_block)
        else:
            operands += [geo, result]
            in_specs += [geo_block, ANY]
            out_shape.append(shape(*tile))
            out_specs.append(block(tile, lambda i: (0, 0)))
            aliases = {len(operands) - 1: 0}

        def kernel(*refs, first=first, at=at):
            step_kernel(first, at, *refs)

        result, last = pl.pallas_call(
            kernel,
            grid=(count,),
            out_shape=out_shape,
            in_specs=in_specs,
            out_specs=out_specs,
            scratch_shapes=[scratch(TILES, HEIGHT, LANES)] * 2 + [scratch(TILES, DIRS * PITCH, LANES)],
            input_output_aliases=aliases,
            compiler_params=params,
            cost_estimate=pl.CostEstimate(flops=1000, bytes_accessed=1000, transcendentals=0),
            name=f"steps_{c}",
        )(*operands)
        token = (last,)
        if first:
            geo = last
        start += count
    return result


def solution(mesh):
    in_specs = (
        P("ens", ("region", "bin"), "pt"),
        P(("ens", "region", "bin"), "pt"),
        P(("ens", "region", "bin"), "pt"),
        P("region", "pt"),
        P("region", "pt"),
        P("region", "pt"),
        P("region", "pt"),
    )
    out_specs = P("ens", ("region", "bin"), "pt")
    return jax.shard_map(
        per_device, mesh=mesh, in_specs=in_specs, out_specs=out_specs, check_vma=False
    )
```

profile of v0, /device:TPU:2, one launch (start us, length us, event | category | flops | bytes accessed | tf_op | source)
XLA Modules:
  0.0 62.3 jit_solution(5799004602900703529)
XLA Ops:
  0.0 3.1 %head.1 = (f32[2,432,8,128]{3,2,1,0:T(8,128)S(1)}, f32[2,1728,128]{2,1,0:T(8,128)S(1)}, f32[2,36,8,128]{3,2,1,0:T(8,128)S(1)}, f32[2,8,128]{2,1,0:T(8,128)S(1)},...) custom-call(f32[432,8,256]{2,1,0:T(8,128)} %spec.1, f32[8,256]{1,0:T(8,128)} %u_hbm.1, ...), custom_call_target="tpu_custom_call" | custom-call | flops 1000 | bytes 1000 | tf_op jit(solution)/shard_map/head/pallas_call | solution.py:405
  3.1 3.5 %collective-permute-start = (f32[496,256]{1,0:T(8,128)S(1)}, f32[496,256]{1,0:T(8,128)S(1)}, u32[]{:S(2)}, u32[]{:S(2)}) collective-permute-start(f32[496,256]{1,0:T(8,128)S(1)} %get-tuple-element.36), channel_id=1, source_target_pairs={{0,2},{2,4},{4,6},{6,8},{8,10},{10,12},{12,14},{1,3},{3,5},{5,7},{... | collective-permute-start | bytes 1523720 | tf_op jit(solution)/shard_map/ppermute | solution.py:446
  6.6 2.4 %collective-permute-start.1 = (f32[496,256]{1,0:T(8,128)S(1)}, f32[496,256]{1,0:T(8,128)S(1)}, u32[]{:S(2)}, u32[]{:S(2)}) collective-permute-start(f32[496,256]{1,0:T(8,128)S(1)} %get-tuple-element.37), channel_id=1, source_target_pairs={{2,0},{4,2},{6,4},{8,6},{10,8},{12,10},{14,12},{3,1},{5,3},{7,5},{... | collective-permute-start | bytes 1523720 | tf_op jit(solution)/shard_map/ppermute | solution.py:447
  9.0 2.3 %rest.1 = (f32[2,1728,128]{2,1,0:T(8,128)S(1)}, f32[312,128]{1,0:T(8,128)S(1)}, f32[320,256]{1,0:T(8,128)S(1)}, f32[160,256]{1,0:T(8,128)S(1)}, f32[320,256]{1,0:T(8,128)S(1)}, /*index=5*/f32[160,256]{1,0:T(8,128)S(1)}) custom-call(f32[2,432,8,128]{3,2,1,0:T(8,128)S(1)} %get-tuple-element.29.raw, f32[2,1728,128]{2,1,0:T(8,128)S(1)} %get-tuple-element.30.src0.refs_0_, ...), custom_call_target="tpu_custom_call" | custom-call | flops 1000 | bytes 1000 | tf_op jit(solution)/shard_map/rest/pallas_call | solution.py:426
  11.3 0.1 collective-permute-start.2
  11.4 1.4 %collective-permute-done.2.other = f32[312,128]{1,0:T(8,128)S(1)} collective-permute-done((f32[312,128]{1,0:T(8,128)S(1)}, f32[312,128]{1,0:T(8,128)S(1)}, u32[]{:S(2)}, u32[]{:S(2)}) %collective-permute-start.2) | collective-permute-done | bytes 159776 | tf_op jit(solution)/shard_map/ppermute | solution.py:450
  12.8 4.3 %collective-permute-start.3 = (f32[96,128]{1,0:T(8,128)S(1)}, f32[96,128]{1,0:T(8,128)S(1)}, u32[]{:S(2)}, u32[]{:S(2)}) collective-permute-start(f32[96,128]{1,0:T(8,128)S(1)} %get-tuple-element.40), channel_id=1, source_target_pairs={{0,2},{2,4},{4,6},{6,8},{8,10},{10,12},{12,14},{1,3},{3,5},{5,7},{... | collective-permute-start | bytes 147464 | tf_op jit(solution)/shard_map/ppermute | solution.py:446
  17.1 1.9 %collective-permute-start.4 = (f32[96,128]{1,0:T(8,128)S(1)}, f32[96,128]{1,0:T(8,128)S(1)}, u32[]{:S(2)}, u32[]{:S(2)}) collective-permute-start(f32[96,128]{1,0:T(8,128)S(1)} %get-tuple-element.41), channel_id=1, source_target_pairs={{2,0},{4,2},{6,4},{8,6},{10,8},{12,10},{14,12},{3,1},{5,3},{7,5},{... | collective-permute-start | bytes 147464 | tf_op jit(solution)/shard_map/ppermute | solution.py:447
  19.0 12.3 %collective-permute-done.3.up = f32[96,128]{1,0:T(8,128)S(1)} collective-permute-done((f32[96,128]{1,0:T(8,128)S(1)}, f32[96,128]{1,0:T(8,128)S(1)}, u32[]{:S(2)}, u32[]{:S(2)}) %collective-permute-start.3) | collective-permute-done | bytes 49184 | tf_op jit(solution)/shard_map/ppermute | solution.py:446
  31.3 0.0 collective-permute-done.4.down
  31.3 4.3 %collective-permute-start.7 = (f32[320,256]{1,0:T(8,128)S(1)}, f32[320,256]{1,0:T(8,128)S(1)}, u32[]{:S(2)}, u32[]{:S(2)}) collective-permute-start(f32[320,256]{1,0:T(8,128)S(1)} %get-tuple-element.47), channel_id=1, source_target_pairs={{0,2},{2,4},{4,6},{6,8},{8,10},{10,12},{12,14},{1,3},{3,5},{5,7},{... | collective-permute-start | bytes 983048 | tf_op jit(solution)/shard_map/ppermute | solution.py:446
  35.7 1.9 %collective-permute-start.8 = (f32[320,256]{1,0:T(8,128)S(1)}, f32[320,256]{1,0:T(8,128)S(1)}, u32[]{:S(2)}, u32[]{:S(2)}) collective-permute-start(f32[320,256]{1,0:T(8,128)S(1)} %get-tuple-element.49), channel_id=1, source_target_pairs={{2,0},{4,2},{6,4},{8,6},{10,8},{12,10},{14,12},{3,1},{5,3},{7,5},{... | collective-permute-start | bytes 983048 | tf_op jit(solution)/shard_map/ppermute | solution.py:447
  37.6 0.4 border.1.refs_3_
  38.0 0.0 collective-permute-done.refs_1_.refs_5_
  38.1 0.0 collective-permute-done.1.refs_2_.refs_6_
  38.1 8.1 %steps_0.1 = (f32[432,8,256]{2,1,0:T(8,128)}, f32[3,2,16,128]{3,2,1,0:T(8,128)S(1)}) custom-call(f32[2,1728,128]{2,1,0:T(8,128)S(1)} %get-tuple-element.30.src0.refs_0_, f32[496,256]{1,0:T(8,128)S(1)} %collective-permute-done.refs_1_.refs_5_, f32[496,256]{1,0:T(8,128)S(1)} %collective-permute-done.1.refs_2_.refs_6_, f32[4,592,128]{2,1,0:T(8,128)S(1)} %border.1.refs_3_, ...), custom_call_target="tpu_custom_call" | custom-call | flops 1000 | bytes 1000 | tf_op jit(solution)/shard_map/steps_0/pallas_call | solution.py:513
  46.2 4.8 %collective-permute-start.5 = (f32[160,256]{1,0:T(8,128)S(1)}, f32[160,256]{1,0:T(8,128)S(1)}, u32[]{:S(2)}, u32[]{:S(2)}) collective-permute-start(f32[160,256]{1,0:T(8,128)S(1)} %get-tuple-element.43), channel_id=1, source_target_pairs={{0,2},{2,4},{4,6},{6,8},{8,10},{10,12},{12,14},{1,3},{3,5},{5,7},{... | collective-permute-start | bytes 491528 | tf_op jit(solution)/shard_map/ppermute | solution.py:446
  51.0 1.9 %collective-permute-start.6 = (f32[160,256]{1,0:T(8,128)S(1)}, f32[160,256]{1,0:T(8,128)S(1)}, u32[]{:S(2)}, u32[]{:S(2)}) collective-permute-start(f32[160,256]{1,0:T(8,128)S(1)} %get-tuple-element.45), channel_id=1, source_target_pairs={{2,0},{4,2},{6,4},{8,6},{10,8},{12,10},{14,12},{3,1},{5,3},{7,5},{... | collective-permute-start | bytes 491528 | tf_op jit(solution)/shard_map/ppermute | solution.py:447
  52.9 0.0 collective-permute-done.7.refs_1_
  52.9 0.0 collective-permute-done.8.refs_2_
  52.9 5.6 %steps_1.1 = (f32[432,8,256]{2,1,0:T(8,128)}, f32[8,128]{1,0:T(8,128)}) custom-call(f32[2,1728,128]{2,1,0:T(8,128)S(1)} %get-tuple-element.34.refs_0_, f32[320,256]{1,0:T(8,128)S(1)} %collective-permute-done.7.refs_1_, f32[320,256]{1,0:T(8,128)S(1)} %collective-permute-done.8.refs_2_, ...), custom_call_target="tpu_custom_call", output_to_operand_aliasing={{0}: (5, {})} | custom-call | flops 1000 | bytes 1000 | tf_op jit(solution)/shard_map/steps_1/pallas_call | solution.py:513
  58.5 0.0 collective-permute-done.5.refs_1_
  58.5 0.5 collective-permute-done.6.refs_2_
  59.1 3.2 %steps_2.1 = (f32[432,8,256]{2,1,0:T(8,128)}, f32[8,128]{1,0:T(8,128)}) custom-call(f32[2,1728,128]{2,1,0:T(8,128)S(1)} %get-tuple-element.34.refs_0_, f32[160,256]{1,0:T(8,128)S(1)} %collective-permute-done.5.refs_1_, f32[160,256]{1,0:T(8,128)S(1)} %collective-permute-done.6.refs_2_, ...), custom_call_target="tpu_custom_call", output_to_operand_aliasing={{0}: (5, {})} | custom-call | flops 1000 | bytes 1000 | tf_op jit(solution)/shard_map/steps_2/pallas_call | solution.py:513
  (1 shorter events, 0.0 us)
Async XLA Ops:
  3.1 34.9 %collective-permute-start = (f32[496,256]{1,0:T(8,128)S(1)}, f32[496,256]{1,0:T(8,128)S(1)}, u32[]{:S(2)}, u32[]{:S(2)}) collective-permute-start(f32[496,256]{1,0:T(8,128)S(1)} %get-tuple-element.36), channel_id=1, source_target_pairs={{0,2},{2,4},{4,6},{6,8},{8,10},{10,12},{12,14},{1,3},{3,5},{5,7},{... | collective-permute-start | bytes 1523720 | tf_op jit(solution)/shard_map/ppermute | solution.py:446
  6.6 31.5 %collective-permute-start.1 = (f32[496,256]{1,0:T(8,128)S(1)}, f32[496,256]{1,0:T(8,128)S(1)}, u32[]{:S(2)}, u32[]{:S(2)}) collective-permute-start(f32[496,256]{1,0:T(8,128)S(1)} %get-tuple-element.37), channel_id=1, source_target_pairs={{2,0},{4,2},{6,4},{8,6},{10,8},{12,10},{14,12},{3,1},{5,3},{7,5},{... | collective-permute-start | bytes 1523720 | tf_op jit(solution)/shard_map/ppermute | solution.py:447
  11.3 1.5 %collective-permute-start.2 = (f32[312,128]{1,0:T(8,128)S(1)}, f32[312,128]{1,0:T(8,128)S(1)}, u32[]{:S(2)}, u32[]{:S(2)}) collective-permute-start(f32[312,128]{1,0:T(8,128)S(1)} %get-tuple-element.38.own), channel_id=1, source_target_pairs={{0,1},{1,0},{2,3},{3,2},{4,5},{5,4},{6,7},{7,6},{8,9},{9,8},{10,11... | collective-permute-start | bytes 479240 | tf_op jit(solution)/shard_map/ppermute | solution.py:450
  12.8 18.5 %collective-permute-start.3 = (f32[96,128]{1,0:T(8,128)S(1)}, f32[96,128]{1,0:T(8,128)S(1)}, u32[]{:S(2)}, u32[]{:S(2)}) collective-permute-start(f32[96,128]{1,0:T(8,128)S(1)} %get-tuple-element.40), channel_id=1, source_target_pairs={{0,2},{2,4},{4,6},{6,8},{8,10},{10,12},{12,14},{1,3},{3,5},{5,7},{... | collective-permute-start | bytes 147464 | tf_op jit(solution)/shard_map/ppermute | solution.py:446
  17.1 14.2 %collective-permute-start.4 = (f32[96,128]{1,0:T(8,128)S(1)}, f32[96,128]{1,0:T(8,128)S(1)}, u32[]{:S(2)}, u32[]{:S(2)}) collective-permute-start(f32[96,128]{1,0:T(8,128)S(1)} %get-tuple-element.41), channel_id=1, source_target_pairs={{2,0},{4,2},{6,4},{8,6},{10,8},{12,10},{14,12},{3,1},{5,3},{7,5},{... | collective-permute-start | bytes 147464 | tf_op jit(solution)/shard_map/ppermute | solution.py:447
  31.3 21.6 %collective-permute-start.7 = (f32[320,256]{1,0:T(8,128)S(1)}, f32[320,256]{1,0:T(8,128)S(1)}, u32[]{:S(2)}, u32[]{:S(2)}) collective-permute-start(f32[320,256]{1,0:T(8,128)S(1)} %get-tuple-element.47), channel_id=1, source_target_pairs={{0,2},{2,4},{4,6},{6,8},{8,10},{10,12},{12,14},{1,3},{3,5},{5,7},{... | collective-permute-start | bytes 983048 | tf_op jit(solution)/shard_map/ppermute | solution.py:446
  35.7 17.3 %collective-permute-start.8 = (f32[320,256]{1,0:T(8,128)S(1)}, f32[320,256]{1,0:T(8,128)S(1)}, u32[]{:S(2)}, u32[]{:S(2)}) collective-permute-start(f32[320,256]{1,0:T(8,128)S(1)} %get-tuple-element.49), channel_id=1, source_target_pairs={{2,0},{4,2},{6,4},{8,6},{10,8},{12,10},{14,12},{3,1},{5,3},{7,5},{... | collective-permute-start | bytes 983048 | tf_op jit(solution)/shard_map/ppermute | solution.py:447
  46.2 12.4 %collective-permute-start.5 = (f32[160,256]{1,0:T(8,128)S(1)}, f32[160,256]{1,0:T(8,128)S(1)}, u32[]{:S(2)}, u32[]{:S(2)}) collective-permute-start(f32[160,256]{1,0:T(8,128)S(1)} %get-tuple-element.43), channel_id=1, source_target_pairs={{0,2},{2,4},{4,6},{6,8},{8,10},{10,12},{12,14},{1,3},{3,5},{5,7},{... | collective-permute-start | bytes 491528 | tf_op jit(solution)/shard_map/ppermute | solution.py:446
  51.0 8.1 %collective-permute-start.6 = (f32[160,256]{1,0:T(8,128)S(1)}, f32[160,256]{1,0:T(8,128)S(1)}, u32[]{:S(2)}, u32[]{:S(2)}) collective-permute-start(f32[160,256]{1,0:T(8,128)S(1)} %get-tuple-element.45), channel_id=1, source_target_pairs={{2,0},{4,2},{6,4},{8,6},{10,8},{12,10},{14,12},{3,1},{5,3},{7,5},{... | collective-permute-start | bytes 491528 | tf_op jit(solution)/shard_map/ppermute | solution.py:447
where the time goes:
time: 63.4 us; the launch traced here: 62.3 us
  starting transfers between devices  25.2 us (40%)
  Pallas kernels  22.8 us (36%)
  waiting for transfers between devices  14.2 us (22%)
    ppermute x4, starting transfers between devices, per_device(): send_up = lambda x: lax.ppermute(x, ('region', 'bin'), up_pairs)  16.9 us
    pallas_call x3, Pallas kernels, per_device(): pl.pallas_call(kernel, grid=(count,), out_shape=out_shape, in_specs=in_sp...  16.9 us
    ppermute x4, waiting for transfers between devices, per_device(): send_up = lambda x: lax.ppermute(x, ('region', 'bin'), up_pairs)  12.3 us
    ppermute x4, starting transfers between devices, per_device(): send_down = lambda x: lax.ppermute(x, ('region', 'bin'), down_pairs)  8.18 us
    pallas_call x1, Pallas kernels, per_device(): pl.pallas_call(head_kernel, out_shape=[shape(TILES, nbins, *tile), shape(...  3.1 us
    pallas_call x1, Pallas kernels, per_device(): pl.pallas_call(rest_kernel, out_shape=[shape(TILES, (F - CHUNKS[0]) * SPA...  2.28 us
    ppermute x1, waiting for transfers between devices, per_device(): other = lax.ppermute(edge, 'pt', [(0, 1), (1, 0)])  1.38 us
  transfers between devices with their start and end apart: 9, of which 3 were waited for; matrix products, arithmetic and copies ran while one was open for 0% of the time, Pallas kernels for 26%

commit v1 on v0

v1 whole, which is shorter than its diff:
```python
import math

import jax
import jax.numpy as jnp
import numpy as np
from jax import lax
from jax.experimental import pallas as pl
from jax.experimental.pallas import tpu as pltpu
from jax.sharding import PartitionSpec as P

F = 12
DIRS = 36
SUB = 4
ROWS = 8
LANES = 128
TILES = 2
HALF = DIRS // 2
SENT = [HALF - 1 + 2 * (SUB - k) for k in range(1, SUB + 1)]
PACK = sum(SENT)
GEO = 16
CHUNKS = (4, 2, 4, 2)
STRIP = 2 * SUB + 2
EDGES = DIRS + 3
TAIL = 48
PITCH = ROWS + 2 * SUB
PAD = 8
HEIGHT = DIRS * PITCH + 2 * PAD
SPAN = DIRS * ROWS

SIGMA = 0.6 * 1.1 ** np.arange(F, dtype=np.float64)
WEIGHT = SIGMA / (DIRS * SIGMA.sum())


def quarter_exact(fn):
    values = np.array([fn(2.0 * math.pi * d / DIRS) for d in range(DIRS)])
    values[np.abs(values) < 1e-9] = 0.0
    return [float(x) for x in values]


COS = quarter_exact(math.cos)
SIN = quarter_exact(math.sin)
SPEED = 0.27 / SIGMA


def of_freq(values, f):
    if isinstance(f, int):
        return float(values[f])
    out = jnp.float32(values[0])
    for i in range(1, F):
        out = jnp.where(f == i, jnp.float32(values[i]), out)
    return out


HBM = pl.BlockSpec(memory_space=pltpu.HBM)
VMEM = pl.BlockSpec(memory_space=pltpu.VMEM)
ANY = pl.BlockSpec(memory_space=pl.ANY)


def segments(up):
    out, row = [], 0
    for k in range(1, SUB + 1):
        low = 1 - (SUB - k) + (0 if up else HALF)
        left, at = SENT[k - 1], low
        while left > 0:
            first = at % DIRS
            count = min(left, DIRS - first)
            out.append((k, first, count, row))
            row, at, left = row + count, at + count, left - count
    return out


def lane_iota():
    return lax.broadcasted_iota(jnp.int32, (ROWS, LANES), 1)


def own_lanes():
    own = jnp.zeros((ROWS, LANES), jnp.bool_)
    for f in range(F):
        own = own | (lane_iota() == f * STRIP + SUB) | (lane_iota() == f * STRIP + SUB + 1)
    return own


def put_edges(pairs):
    lanes = lane_iota()
    packed = jnp.zeros((ROWS, LANES), jnp.float32)
    for f, (first_tile, last_tile) in enumerate(pairs):
        ends = jnp.where(lanes < LANES // 2, first_tile, last_tile)
        at = f * STRIP
        packed = jnp.where(lanes >= at, pltpu.roll(ends, (at + SUB) % LANES, 1), packed)
        packed = jnp.where(lanes >= at + SUB + 1, pltpu.roll(ends, (at + SUB + 2) % LANES, 1), packed)
    return packed


def split(value):
    return value[:, :LANES], value[:, LANES:]


def make_sources(raw, src, push, inverse, f, base):
    sig = of_freq(SIGMA, f)
    for t in range(TILES):
        for d in range(DIRS):
            grown = raw[t, f * DIRS + d] * (1.0 + sig * push[t, d])
            row = base + d * ROWS
            src[t, pl.ds(row, ROWS), :] = grown * inverse[t]


def make_packs(src, base, local, up_ref, down_ref):
    for ref, up in ((up_ref, True), (down_ref, False)):
        for k, d0, count, row in segments(up):
            j = ROWS - k if up else k - 1
            for t in range(TILES):
                ref[t, pl.ds(local * PACK + row, count), :] = src[t, pl.ds(base + d0 * ROWS + j, count, stride=ROWS), :]


def head_kernel(
    spec, u_hbm, v_hbm, mask_hbm, depth_hbm, sx_hbm, sy_hbm,
    raw, src0, push, damp_ref, geo, up_ref, down_ref,
    u_ref, v_ref, mask_ref, depth_ref, sx_ref, sy_ref, small_sem, in_sem,
):
    off = pl.multiple_of(lax.axis_index("bin") * ROWS, ROWS)
    own = pl.ds(off, ROWS)
    small = [
        pltpu.make_async_copy(a, b, small_sem.at[i])
        for i, (a, b) in enumerate(
            (
                (u_hbm, u_ref),
                (v_hbm, v_ref),
                (mask_hbm.at[own], mask_ref),
                (depth_hbm.at[own], depth_ref),
                (sx_hbm.at[own], sx_ref),
                (sy_hbm.at[own], sy_ref),
            )
        )
    ]

    def load(f, t):
        return pltpu.make_async_copy(
            spec.at[pl.ds(f * DIRS, DIRS), :, pl.ds(t * LANES, LANES)],
            raw.at[t, pl.ds(f * DIRS, DIRS)],
            in_sem.at[f, t],
        )

    for copy in small:
        copy.start()
    for f in range(F):
        for t in range(TILES):
            load(f, t).start()
    for copy in small:
        copy.wait()

    mask = mask_ref[...].astype(jnp.float32)
    fields = (depth_ref[...] * mask, sx_ref[...] * mask, sy_ref[...] * mask)
    tail = CHUNKS[0] * PACK
    for g in range(3):
        for t, tile in enumerate(split(fields[g])):
            geo[g, t] = tile
        rows = slice(tail + g * SUB, tail + (g + 1) * SUB)
        for t, tile in enumerate(split(fields[g])):
            up_ref[t, rows, :] = tile[ROWS - SUB :, :]
            down_ref[t, rows, :] = tile[:SUB, :]
    for ref in (up_ref, down_ref):
        for t in range(TILES):
            ref[t, tail + 3 * SUB :, :] = jnp.zeros((GEO - 3 * SUB, LANES), jnp.float32)
    for t, tile in enumerate(split(mask)):
        geo[3, t] = tile
    u, v = split(u_ref[...]), split(v_ref[...])
    for d in range(DIRS):
        for t in range(TILES):
            lean = jnp.maximum(u[t] * COS[d] + v[t] * SIN[d], 0.0)
            push[t, d] = 0.5 * lean * lean

    zero = jnp.zeros((ROWS, LANES), jnp.float32)
    sums = [(zero, zero)] * TILES
    for f in range(F):
        for t in range(TILES):
            load(f, t).wait()
            parts = [raw[t, f * DIRS + d] for d in range(4)]
            for d in range(4, DIRS):
                parts[d % 4] = parts[d % 4] + raw[t, f * DIRS + d]
            total = (parts[0] + parts[1]) + (parts[2] + parts[3])
            energy, first = sums[t]
            sums[t] = energy + float(WEIGHT[f]) * total, first + float(WEIGHT[f] * SIGMA[f]) * total
    damps = []
    for t, (energy, first) in enumerate(sums):
        mean_sigma = first / energy
        steep = energy * mean_sigma * mean_sigma / 1.5
        damps.append(0.5 * steep * steep / mean_sigma)
        damp_ref[t] = damps[t]

    def body(f, carry):
        inverse = [geo[3, t] / (1.0 + of_freq(SIGMA, f) * damps[t]) for t in range(TILES)]
        base = pl.multiple_of(f * SPAN, SPAN)
        make_sources(raw, src0, push, inverse, f, base)
        make_packs(src0, base, f, up_ref, down_ref)
        return carry

    lax.fori_loop(0, CHUNKS[0], body, 0)


def rest_kernel(raw, src0, push, damp, geo, *refs):
    n = len(CHUNKS) - 1
    src, edge = refs[:2]
    ups, downs = refs[2 : 2 + n], refs[2 + n :]
    at = CHUNKS[0]
    for c in range(n):
        def body(local, carry, c=c, at=at):
            f = at + local
            inverse = [geo[3, t] / (1.0 + of_freq(SIGMA, f) * damp[t]) for t in range(TILES)]
            base = pl.multiple_of((f - CHUNKS[0]) * SPAN, SPAN)
            make_sources(raw, src, push, inverse, f, base)
            make_packs(src, base, local, ups[c], downs[c])
            return carry

        lax.fori_loop(0, CHUNKS[c + 1], body, 0)
        at += CHUNKS[c + 1]

    def edges(d, carry):
        pairs = []
        for f in range(F):
            ref, local = (src0, f) if f < CHUNKS[0] else (src, f - CHUNKS[0])
            row = pl.ds(pl.multiple_of(local * SPAN + d * ROWS, ROWS), ROWS)
            pairs.append((ref[0, row, :], ref[1, row, :]))
        edge[pl.ds(pl.multiple_of(d * ROWS, ROWS), ROWS), :] = put_edges(pairs)
        return carry

    lax.fori_loop(0, DIRS, edges, 0, unroll=4)
    for g in range(3):
        edge[(DIRS + g) * ROWS : (DIRS + g + 1) * ROWS, :] = put_edges([(geo[g, 0], geo[g, 1])] * F)


def join_kernel(own, other, up_in, down_in, edge, up_out, down_out, tails, sem):
    lanes = own_lanes()
    for d in range(EDGES):
        rows = slice(d * ROWS, (d + 1) * ROWS)
        edge[rows, :] = jnp.where(lanes, own[rows, :], other[rows, :])
    copies = []
    for i, (out, up) in enumerate(((up_out, True), (down_out, False))):
        pieces = [
            (row, count, pl.ds(d0 * ROWS + (ROWS - k if up else k - 1), count, stride=ROWS))
            for k, d0, count, row in segments(up)
        ]
        for g in range(3):
            pieces.append((PACK + g * SUB, SUB, pl.ds((DIRS + g) * ROWS + (ROWS - SUB if up else 0), SUB)))
        for row, count, place in pieces:
            value, at = edge[place, :], 0
            while at < count:
                half, inner = divmod(row + at, TAIL)
                size = min(count - at, TAIL - inner)
                tails[i, half, inner : inner + size, :] = value[at : at + size]
                at += size
        rest = 2 * TAIL - PACK - 3 * SUB
        tails[i, 1, TAIL - rest :, :] = jnp.zeros((rest, LANES), jnp.float32)
        copies.append(
            pltpu.make_async_copy(tails.at[i], out.at[:, pl.ds(CHUNKS[1] * PACK, TAIL)], sem.at[i])
        )
        copies[-1].start()
    for copy in copies:
        copy.wait()


def border_kernel(own, up, down, field):
    zero = jnp.zeros((ROWS, LANES), jnp.float32)
    for s in range(SUB):
        field[s, :PAD, :] = zero
        field[s, HEIGHT - PAD :, :] = zero
    for d in range(DIRS + 1):
        row = PAD + d * PITCH - SUB
        field[0, row : row + 2 * SUB, :] = zero
    for d in range(DIRS):
        row = PAD + d * PITCH + SUB
        field[0, row : row + ROWS, :] = own[d * ROWS : (d + 1) * ROWS, :]
    tail = CHUNKS[1] * PACK
    halves = [
        jnp.concatenate([ref[0, tail : tail + TAIL, :], ref[1, tail : tail + TAIL, :]], axis=0)
        for ref in (up, down)
    ]
    for value, is_up in zip(halves, (True, False)):
        for k, d0, count, row in segments(is_up):
            place = PAD + d0 * PITCH + (SUB - k if is_up else SUB + ROWS + k - 1)
            field[0, pl.ds(place, count, stride=PITCH), :] = value[row : row + count]
    speed = jnp.zeros((ROWS, LANES), jnp.float32)
    for f in range(F):
        speed = jnp.where(lane_iota() >= f * STRIP, float(SPEED[f]), speed)
    coefficients = []
    for half in range(2):
        geo = []
        for g in range(3):
            mine = own[(DIRS + g) * ROWS + half * SUB : (DIRS + g) * ROWS + (half + 1) * SUB, :]
            halo = halves[half][PACK + g * SUB : PACK + (g + 1) * SUB]
            geo.append(speed * jnp.concatenate([mine, halo] if half else [halo, mine], axis=0))
        coefficients.append((geo[0], 0.5 * geo[1], 0.5 * geo[2]))
    for step in range(SUB - 1):
        for half in range(2):
            depth, sx, sy = coefficients[half]

            def load(d, shift=0):
                row = PAD + (d % DIRS) * PITCH + half * ROWS + shift
                return field[step, row : row + ROWS, :]

            for d in range(DIRS):
                west, south = COS[d] >= 0.0, SIN[d] >= 0.0
                cos, sin = abs(COS[d]), abs(SIN[d])
                now = load(d)
                up_x = pltpu.roll(now, 1 if west else LANES - 1, 1)
                up_y = load(d, -1 if south else 1)
                vt = SIN[d] * sx - COS[d] * sy
                up_t = jnp.where(vt > 0.0, load(d - 1), load(d + 1))
                moved = depth * (cos * up_x + sin * up_y - (cos + sin) * now) + jnp.abs(vt) * (up_t - now)
                row = PAD + d * PITCH + half * ROWS
                field[step + 1, row : row + ROWS, :] = now + moved


def step_kernel(first, start, count, source_at, *refs):
    if first:
        src, up, down, border, geo_own, out, geo, field_a, field_b, turn, done, sem = refs
        tail = count * PACK
        for g in range(3):
            rows = slice(tail + g * SUB, tail + (g + 1) * SUB)
            for t in range(TILES):
                geo[g, t, :SUB] = up[t, rows, :]
                geo[g, t, SUB : SUB + ROWS] = geo_own[g, t]
                geo[g, t, SUB + ROWS :] = down[t, rows, :]
    else:
        src, up, down, border, geo, _, out, field_a, field_b, turn, done, sem = refs
    zero = jnp.zeros((ROWS, LANES), jnp.float32)
    for t in range(TILES):
        for field in (field_a, field_b):
            field[t, :PAD, :] = zero
            field[t, HEIGHT - PAD :, :] = zero
        for d in range(DIRS + 1):
            row = PAD + d * PITCH - SUB
            field_a[t, row : row + 2 * SUB, :] = zero
        for half in range(2):
            rows = slice(half * ROWS, (half + 1) * ROWS)
            sx, sy = 0.5 * geo[1, t, rows], 0.5 * geo[2, t, rows]
            for d in range(DIRS):
                turn[t, d * PITCH + half * ROWS : d * PITCH + (half + 1) * ROWS, :] = SIN[d] * sx - COS[d] * sy
    lanes = lane_iota()
    at_first, at_last = lanes == 0, lanes == LANES - 1
    quarter = DIRS // 4

    def put(i, q):
        slot = lax.rem(i, 2)
        return pltpu.make_async_copy(
            done.at[slot, pl.ds(q * quarter, quarter)],
            out.at[pl.ds((start + i) * DIRS + q * quarter, quarter)],
            sem.at[slot, q],
        )

    def frequency(i, carry):
        base = pl.multiple_of((source_at + i) * SPAN, SPAN)
        for d in range(DIRS):
            row = PAD + d * PITCH + SUB
            for t in range(TILES):
                field_a[t, row : row + ROWS, :] = src[t, pl.ds(base + d * ROWS, ROWS), :]
        for ref, is_up in ((up, True), (down, False)):
            for k, d0, number, row in segments(is_up):
                place = PAD + d0 * PITCH + (SUB - k if is_up else SUB + ROWS + k - 1)
                place = pl.ds(place, number, stride=PITCH)
                for t in range(TILES):
                    field_a[t, place, :] = ref[t, pl.ds(i * PACK + row, number), :]

        freq = start + i
        speed = of_freq(SPEED, freq)
        to_first = LANES - (freq * STRIP + SUB - 1)
        to_last = LANES - 1 - (freq * STRIP + SUB + 2)

        @pl.when(i >= 2)
        def _():
            for q in range(4):
                put(i - 2, q).wait()

        def advance(step, old, new):
            last = step == SUB - 1
            for part in (SUB,) if last else (0, ROWS):
                depth = [speed * geo[0, t, part : part + ROWS] for t in range(TILES)]

                def load(d, shift=0):
                    row = PAD + (d % DIRS) * PITCH + part + shift
                    return [old[t, row : row + ROWS, :] for t in range(TILES)]

                before, now = load(-1), load(0)
                initial = now
                for d in range(DIRS):
                    after = load(d + 1) if d < DIRS - 1 else initial
                    west, south = COS[d] >= 0.0, SIN[d] >= 0.0
                    cos, sin = abs(COS[d]), abs(SIN[d])
                    row = PAD + d * PITCH + part
                    outer = pltpu.roll(border[step, row : row + ROWS, :], to_first if west else to_last, 1)
                    rolled = [pltpu.roll(x, 1 if west else LANES - 1, 1) for x in now]
                    up_y = load(d, -1 if south else 1)
                    for t in range(TILES):
                        if west:
                            up_x = jnp.where(at_first, rolled[t - 1] if t else outer, rolled[t])
                        else:
                            up_x = jnp.where(at_last, rolled[t + 1] if t < TILES - 1 else outer, rolled[t])
                        vt = turn[t, d * PITCH + part : d * PITCH + part + ROWS, :]
                        up_t = jnp.where(vt > 0.0, before[t], after[t])
                        moved = depth[t] * (cos * up_x + sin * up_y[t] - (cos + sin) * now[t])
                        value = now[t] + (moved + speed * jnp.abs(vt) * (up_t - now[t]))
                        if last:
                            done[lax.rem(i, 2), d, :, t * LANES : (t + 1) * LANES] = value
                        else:
                            new[t, row : row + ROWS, :] = value
                    before, now = now, after
                    if last and d % quarter == quarter - 1:
                        put(i, d // quarter).start()

        fields = (field_a, field_b)
        for step in range(SUB):
            advance(step, fields[step % 2], fields[(step + 1) % 2])
        return carry

    lax.fori_loop(0, count, frequency, 0)
    for i in range(max(count - 2, 0), count):
        for q in range(4):
            put(i, q).wait()


def after(value, *others):
    return lax.optimization_barrier((value, *others))[0]


def per_device(spectrum, wind_u, wind_v, sea_mask, depth_factor, slope_x, slope_y):
    nbins, rows, cols = spectrum.shape
    assert (nbins, rows, cols) == (F * DIRS, ROWS, TILES * LANES)
    assert lax.axis_size("pt") == 2
    f32 = jnp.float32
    shape = lambda *s: jax.ShapeDtypeStruct(s, f32)
    scratch = lambda *s: pltpu.VMEM(s, f32)
    heights = [c * PACK + (GEO, TAIL, 0, 0)[min(i, 2)] for i, c in enumerate(CHUNKS)]
    params = pltpu.CompilerParams(vmem_limit_bytes=32 * 2**20)
    cost = pl.CostEstimate(flops=1000, bytes_accessed=1000, transcendentals=0)
    tile = (rows, LANES)

    pinned = [
        pltpu.with_memory_space_constraint(x, pltpu.HBM)
        for x in (spectrum, wind_u, wind_v, sea_mask, depth_factor, slope_x, slope_y)
    ]
    raw, src0, push, damp, geo_own, up0, down0 = pl.pallas_call(
        head_kernel,
        out_shape=[
            shape(TILES, nbins, *tile),
            shape(TILES, CHUNKS[0] * SPAN, LANES),
            shape(TILES, DIRS, *tile),
            shape(TILES, *tile),
            shape(4, TILES, *tile),
            shape(TILES, heights[0], LANES),
            shape(TILES, heights[0], LANES),
        ],
        in_specs=[HBM] * 7,
        out_specs=[VMEM] * 7,
        scratch_shapes=[pltpu.VMEM((rows, cols), x.dtype) for x in (wind_u, wind_v, sea_mask, depth_factor, slope_x, slope_y)]
        + [pltpu.SemaphoreType.DMA((6,)), pltpu.SemaphoreType.DMA((F, TILES))],
        compiler_params=params,
        cost_estimate=cost,
        name="head",
    )(*pinned)

    n = len(CHUNKS) - 1
    outs = pl.pallas_call(
        rest_kernel,
        out_shape=[
            shape(TILES, (F - CHUNKS[0]) * SPAN, LANES),
            shape(EDGES * rows, LANES),
            *[shape(TILES, h, LANES) for h in heights[1:]] * 2,
        ],
        in_specs=[VMEM] * 5,
        out_specs=[VMEM] * (2 + 2 * n),
        compiler_params=params,
        cost_estimate=cost,
        name="rest",
    )(raw, src0, push, damp, geo_own)
    src, edge = outs[:2]
    ups, downs = [up0, *outs[2 : 2 + n]], [down0, *outs[2 + n :]]

    blocks = lax.axis_size("region") * lax.axis_size("bin")
    up_pairs = [(i, i + 1) for i in range(blocks - 1)]
    down_pairs = [(j, i) for i, j in up_pairs]
    send_up = lambda x: lax.ppermute(x, ("region", "bin"), up_pairs)
    send_down = lambda x: lax.ppermute(x, ("region", "bin"), down_pairs)

    from_south, from_north = [send_up(ups[0])], [send_down(downs[0])]
    other = lax.ppermute(edge, "pt", [(0, 1), (1, 0)])
    edge, ups[1], downs[1] = pl.pallas_call(
        join_kernel,
        out_shape=[shape(EDGES * rows, LANES), shape(TILES, heights[1], LANES), shape(TILES, heights[1], LANES)],
        in_specs=[VMEM, VMEM, ANY, ANY],
        out_specs=[VMEM, ANY, ANY],
        scratch_shapes=[scratch(2, TILES, TAIL, LANES), pltpu.SemaphoreType.DMA((2,))],
        input_output_aliases={2: 1, 3: 2},
        compiler_params=params,
        cost_estimate=cost,
        name="join",
    )(edge, other, ups[1], downs[1])
    wait = (from_south[0], from_north[0])
    from_south += [send_up(ups[1]), send_up(after(ups[2], *wait))]
    from_north += [send_down(downs[1]), send_down(after(downs[2], *wait))]
    border = pl.pallas_call(
        border_kernel,
        out_shape=shape(SUB, HEIGHT, LANES),
        in_specs=[VMEM] * 3,
        out_specs=VMEM,
        compiler_params=params,
        cost_estimate=cost,
        name="border",
    )(edge, from_south[1], from_north[1])


    start, geo, result = 0, None, None
    for c, count in enumerate(CHUNKS):
        first = c == 0
        operands = [src0 if first else src, from_south[c], from_north[c], border]
        in_specs = [VMEM] * 5
        out_shape = [shape(nbins, rows, cols)]
        aliases = {}
        if first:
            operands.append(geo_own)
            out_shape.append(shape(3, TILES, PITCH, LANES))
        else:
            operands += [geo, result]
            in_specs.append(ANY)
            aliases = {len(operands) - 1: 0}

        def kernel(*refs, first=first, start=start, count=count):
            step_kernel(first, start, count, start - (0 if first else CHUNKS[0]), *refs)

        outs = pl.pallas_call(
            kernel,
            out_shape=out_shape,
            in_specs=in_specs,
            out_specs=[ANY, VMEM][: len(out_shape)],
            scratch_shapes=[scratch(TILES, HEIGHT, LANES)] * 2
            + [scratch(TILES, DIRS * PITCH, LANES), scratch(2, DIRS, rows, cols), pltpu.SemaphoreType.DMA((2, 4))],
            input_output_aliases=aliases,
            compiler_params=params,
            cost_estimate=cost,
            name=f"steps_{c}",
        )(*operands)
        result = outs[0]
        if first:
            geo = outs[1]
            for later in range(3, len(CHUNKS)):
                from_south.append(send_up(after(ups[later], geo)))
                from_north.append(send_down(after(downs[later], geo)))
        start += count
    return result


def solution(mesh):
    in_specs = (
        P("ens", ("region", "bin"), "pt"),
        P(("ens", "region", "bin"), "pt"),
        P(("ens", "region", "bin"), "pt"),
        P("region", "pt"),
        P("region", "pt"),
        P("region", "pt"),
        P("region", "pt"),
    )
    out_specs = P("ens", ("region", "bin"), "pt")
    return jax.shard_map(
        per_device, mesh=mesh, in_specs=in_specs, out_specs=out_specs, check_vma=False
    )
```

time: 63.4 us -> 59.7 us (0.942)
  the two profiles are of different devices: /device:TPU:2 before, /device:TPU:9 now
where the time goes in v1:
time: 59.7 us; the launch traced here: 59.4 us
  starting transfers between devices  26 us (44%)
  Pallas kernels  23.5 us (39%)
  waiting for transfers between devices  9.72 us (16%)
    pallas_call x4, Pallas kernels, per_device(): pl.pallas_call(kernel, out_shape=out_shape, in_specs=in_specs, out_specs=...  17.7 us
    ppermute x4, starting transfers between devices, per_device(): send_down = lambda x: lax.ppermute(x, ('region', 'bin'), down_pairs)  15.4 us
    ppermute x4, starting transfers between devices, per_device(): send_up = lambda x: lax.ppermute(x, ('region', 'bin'), up_pairs)  9.28 us
    ppermute x4, waiting for transfers between devices, per_device(): send_down = lambda x: lax.ppermute(x, ('region', 'bin'), down_pairs)  8.68 us
    pallas_call x1, Pallas kernels, per_device(): pl.pallas_call(head_kernel, out_shape=[shape(TILES, nbins, *tile), shape(...  2.84 us
    pallas_call x1, Pallas kernels, per_device(): pl.pallas_call(rest_kernel, out_shape=[shape(TILES, (F - CHUNKS[0]) * SPA...  2.37 us
    ppermute x1, starting transfers between devices, per_device(): other = lax.ppermute(edge, 'pt', [(0, 1), (1, 0)])  1.3 us
  transfers between devices with their start and end apart: 9, of which 3 were waited for; matrix products, arithmetic and copies ran while one was open for 0% of the time, Pallas kernels for 29%

profile of v1, /device:TPU:9, one launch (start us, length us, event | category | flops | bytes accessed | tf_op | source)
XLA Modules:
  0.0 59.4 jit_solution(8512968655934707086)
XLA Ops:
  0.0 2.8 %head.1 = (f32[2,432,8,128]{3,2,1,0:T(8,128)S(1)}, f32[2,1152,128]{2,1,0:T(8,128)S(1)}, f32[2,36,8,128]{3,2,1,0:T(8,128)S(1)}, f32[2,8,128]{2,1,0:T(8,128)S(1)},...) custom-call(f32[432,8,256]{2,1,0:T(8,128)} %spec.1, f32[8,256]{1,0:T(8,128)} %u_hbm.1, ...), custom_call_target="tpu_custom_call" | custom-call | flops 1000 | bytes 1000 | tf_op jit(solution)/shard_map/head/pallas_call | solution.py:440
  2.8 3.1 %collective-permute-start = (f32[2,336,128]{2,1,0:T(8,128)S(1)}, f32[2,336,128]{2,1,0:T(8,128)S(1)}, u32[]{:S(2)}, u32[]{:S(2)}) collective-permute-start(f32[2,336,128]{2,1,0:T(8,128)S(1)} %get-tuple-element.36), channel_id=1, source_target_pairs={{0,2},{2,4},{4,6},{6,8},{8,10},{10,12},{12,14},{1,3},{3,5},{5,7},{... | collective-permute-start | bytes 1032200 | tf_op jit(solution)/shard_map/ppermute | solution.py:480
  6.0 3.1 %collective-permute-start.1 = (f32[2,336,128]{2,1,0:T(8,128)S(1)}, f32[2,336,128]{2,1,0:T(8,128)S(1)}, u32[]{:S(2)}, u32[]{:S(2)}) collective-permute-start(f32[2,336,128]{2,1,0:T(8,128)S(1)} %get-tuple-element.37), channel_id=1, source_target_pairs={{2,0},{4,2},{6,4},{8,6},{10,8},{12,10},{14,12},{3,1},{5,3},{7,5},{... | collective-permute-start | bytes 1032200 | tf_op jit(solution)/shard_map/ppermute | solution.py:481
  9.0 2.4 %rest.1 = (f32[2,2304,128]{2,1,0:T(8,128)S(1)}, f32[312,128]{1,0:T(8,128)S(1)}, f32[2,208,128]{2,1,0:T(8,128)S(1)}, f32[2,320,128]{2,1,0:T(8,128)S(1)}, f32[2,16...) custom-call(f32[2,432,8,128]{3,2,1,0:T(8,128)S(1)} %get-tuple-element., ...), custom_call_target="tpu_custom_call" | custom-call | flops 1000 | bytes 1000 | tf_op jit(solution)/shard_map/rest/pallas_call | solution.py:461
  11.4 1.3 %collective-permute-start.2 = (f32[312,128]{1,0:T(8,128)S(1)}, f32[312,128]{1,0:T(8,128)S(1)}, u32[]{:S(2)}, u32[]{:S(2)}) collective-permute-start(f32[312,128]{1,0:T(8,128)S(1)} %get-tuple-element.38.own), channel_id=1, source_target_pairs={{0,1},{1,0},{2,3},{3,2},{4,5},{5,4},{6,7},{7,6},{8,9},{9,8},{10,11... | collective-permute-start | bytes 479240 | tf_op jit(solution)/shard_map/ppermute | solution.py:484
  12.7 1.0 %collective-permute-done.2.other = f32[312,128]{1,0:T(8,128)S(1)} collective-permute-done((f32[312,128]{1,0:T(8,128)S(1)}, f32[312,128]{1,0:T(8,128)S(1)}, u32[]{:S(2)}, u32[]{:S(2)}) %collective-permute-start.2) | collective-permute-done | bytes 159776 | tf_op jit(solution)/shard_map/ppermute | solution.py:484
  13.7 0.1 join.1
  13.9 2.2 %collective-permute-start.3 = (f32[2,208,128]{2,1,0:T(8,128)S(1)}, f32[2,208,128]{2,1,0:T(8,128)S(1)}, u32[]{:S(2)}, u32[]{:S(2)}) collective-permute-start(f32[2,208,128]{2,1,0:T(8,128)S(1)} %get-tuple-element.42), channel_id=1, source_target_pairs={{0,2},{2,4},{4,6},{6,8},{8,10},{10,12},{12,14},{1,3},{3,5},{5,7},{... | collective-permute-start | bytes 638984 | tf_op jit(solution)/shard_map/ppermute | solution.py:480
  16.1 4.0 %collective-permute-start.4 = (f32[2,208,128]{2,1,0:T(8,128)S(1)}, f32[2,208,128]{2,1,0:T(8,128)S(1)}, u32[]{:S(2)}, u32[]{:S(2)}) collective-permute-start(f32[2,208,128]{2,1,0:T(8,128)S(1)} %get-tuple-element.43), channel_id=1, source_target_pairs={{2,0},{4,2},{6,4},{8,6},{10,8},{12,10},{14,12},{3,1},{5,3},{7,5},{... | collective-permute-start | bytes 638984 | tf_op jit(solution)/shard_map/ppermute | solution.py:481
  20.1 0.0 collective-permute-done.refs_1_
  20.1 7.5 %collective-permute-done.1.refs_2_ = f32[2,336,128]{2,1,0:T(8,128)S(1)} collective-permute-done((f32[2,336,128]{2,1,0:T(8,128)S(1)}, f32[2,336,128]{2,1,0:T(8,128)S(1)}, u32[]{:S(2)}, u32[]{:S(2)}) %collective-permute-start.1) | collective-permute-done | bytes 344096 | tf_op jit(solution)/shard_map/ppermute | solution.py:481
  27.6 1.9 %collective-permute-start.7 = (f32[2,320,128]{2,1,0:T(8,128)S(1)}, f32[2,320,128]{2,1,0:T(8,128)S(1)}, u32[]{:S(2)}, u32[]{:S(2)}) collective-permute-start(f32[2,320,128]{2,1,0:T(8,128)S(1)} %get-tuple-element.49), channel_id=1, source_target_pairs={{0,2},{2,4},{4,6},{6,8},{8,10},{10,12},{12,14},{1,3},{3,5},{5,7},{... | collective-permute-start | bytes 983048 | tf_op jit(solution)/shard_map/ppermute | solution.py:480
  29.5 4.3 %collective-permute-start.8 = (f32[2,320,128]{2,1,0:T(8,128)S(1)}, f32[2,320,128]{2,1,0:T(8,128)S(1)}, u32[]{:S(2)}, u32[]{:S(2)}) collective-permute-start(f32[2,320,128]{2,1,0:T(8,128)S(1)} %get-tuple-element.51), channel_id=1, source_target_pairs={{2,0},{4,2},{6,4},{8,6},{10,8},{12,10},{14,12},{3,1},{5,3},{7,5},{... | collective-permute-start | bytes 983048 | tf_op jit(solution)/shard_map/ppermute | solution.py:481
  33.7 0.0 collective-permute-done.3.up.refs_1_
  33.8 0.0 collective-permute-done.4.down.refs_2_
  33.8 0.4 border.1.refs_3_
  34.2 5.7 %steps_0.1 = (f32[432,8,256]{2,1,0:T(8,128)}, f32[3,2,16,128]{3,2,1,0:T(8,128)S(1)}) custom-call(f32[2,1152,128]{2,1,0:T(8,128)S(1)} %get-tuple-element.30.src0.refs_0_, f32[2,336,128]{2,1,0:T(8,128)S(1)} %collective-permute-done.refs_1_, f32[2,336,128]{2,1,0:T(8,128)S(1)} %collective-permute-done.1.refs_2_, f32[4,592,128]{2,1,0:T(8,128)S(1)} %border.1.refs_3_, ...), custom_call_target="tpu_custom_call" | custom-call | flops 1000 | bytes 1000 | tf_op jit(solution)/shard_map/steps_0/pallas_call | solution.py:528
  39.9 2.0 %collective-permute-start.5 = (f32[2,160,128]{2,1,0:T(8,128)S(1)}, f32[2,160,128]{2,1,0:T(8,128)S(1)}, u32[]{:S(2)}, u32[]{:S(2)}) collective-permute-start(f32[2,160,128]{2,1,0:T(8,128)S(1)} %get-tuple-element.45), channel_id=1, source_target_pairs={{0,2},{2,4},{4,6},{6,8},{8,10},{10,12},{12,14},{1,3},{3,5},{5,7},{... | collective-permute-start | bytes 491528 | tf_op jit(solution)/shard_map/ppermute | solution.py:480
  41.9 4.1 %collective-permute-start.6 = (f32[2,160,128]{2,1,0:T(8,128)S(1)}, f32[2,160,128]{2,1,0:T(8,128)S(1)}, u32[]{:S(2)}, u32[]{:S(2)}) collective-permute-start(f32[2,160,128]{2,1,0:T(8,128)S(1)} %get-tuple-element.47), channel_id=1, source_target_pairs={{2,0},{4,2},{6,4},{8,6},{10,8},{12,10},{14,12},{3,1},{5,3},{7,5},{... | collective-permute-start | bytes 491528 | tf_op jit(solution)/shard_map/ppermute | solution.py:481
  46.1 3.2 %steps_1.1.refs_5_ = f32[432,8,256]{2,1,0:T(8,128)} custom-call(f32[2,2304,128]{2,1,0:T(8,128)S(1)} %get-tuple-element.34.refs_0_, f32[2,208,128]{2,1,0:T(8,128)S(1)} %collective-permute-done.3.up.refs_1_, f32[2,208,128]{2,1,0:T(8,128)S(1)} %collective-permute-done.4.down.refs_2_, f32[4,592,128]{2,1,0:T(8,128)S(1)} %border.1.refs_3_, ...), custom_call_target="tpu_custom_call", output_to_operand_aliasing={{}: (5, {})} | custom-call | flops 1000 | bytes 1000 | tf_op jit(solution)/shard_map/steps_1/pallas_call | solution.py:528
  49.3 0.0 collective-permute-done.7.refs_1_
  49.3 1.2 %collective-permute-done.8.refs_2_ = f32[2,320,128]{2,1,0:T(8,128)S(1)} collective-permute-done((f32[2,320,128]{2,1,0:T(8,128)S(1)}, f32[2,320,128]{2,1,0:T(8,128)S(1)}, u32[]{:S(2)}, u32[]{:S(2)}) %collective-permute-start.8) | collective-permute-done | bytes 327712 | tf_op jit(solution)/shard_map/ppermute | solution.py:481
  50.5 5.6 %steps_2.1.refs_5_ = f32[432,8,256]{2,1,0:T(8,128)} custom-call(f32[2,2304,128]{2,1,0:T(8,128)S(1)} %get-tuple-element.34.refs_0_, f32[2,320,128]{2,1,0:T(8,128)S(1)} %collective-permute-done.7.refs_1_, f32[2,320,128]{2,1,0:T(8,128)S(1)} %collective-permute-done.8.refs_2_, f32[4,592,128]{2,1,0:T(8,128)S(1)} %border.1.refs_3_, ...), custom_call_target="tpu_custom_call", output_to_operand_aliasing={{}: (5, {})} | custom-call | flops 1000 | bytes 1000 | tf_op jit(solution)/shard_map/steps_2/pallas_call | solution.py:528
  56.2 0.0 collective-permute-done.5.refs_1_
  56.2 0.0 collective-permute-done.6.refs_2_
  56.2 3.2 %steps_3.1 = f32[432,8,256]{2,1,0:T(8,128)} custom-call(f32[2,2304,128]{2,1,0:T(8,128)S(1)} %get-tuple-element.34.refs_0_, f32[2,160,128]{2,1,0:T(8,128)S(1)} %collective-permute-done.5.refs_1_, f32[2,160,128]{2,1,0:T(8,128)S(1)} %collective-permute-done.6.refs_2_, f32[4,592,128]{2,1,0:T(8,128)S(1)} %border.1.refs_3_, ...), custom_call_target="tpu_custom_call", output_to_operand_aliasing={{}: (5, {})} | custom-call | flops 1000 | bytes 1000 | tf_op jit(solution)/shard_map/steps_3/pallas_call | solution.py:528
Async XLA Ops:
  2.8 17.2 %collective-permute-start = (f32[2,336,128]{2,1,0:T(8,128)S(1)}, f32[2,336,128]{2,1,0:T(8,128)S(1)}, u32[]{:S(2)}, u32[]{:S(2)}) collective-permute-start(f32[2,336,128]{2,1,0:T(8,128)S(1)} %get-tuple-element.36), channel_id=1, source_target_pairs={{0,2},{2,4},{4,6},{6,8},{8,10},{10,12},{12,14},{1,3},{3,5},{5,7},{... | collective-permute-start | bytes 1032200 | tf_op jit(solution)/shard_map/ppermute | solution.py:480
  6.0 21.6 %collective-permute-start.1 = (f32[2,336,128]{2,1,0:T(8,128)S(1)}, f32[2,336,128]{2,1,0:T(8,128)S(1)}, u32[]{:S(2)}, u32[]{:S(2)}) collective-permute-start(f32[2,336,128]{2,1,0:T(8,128)S(1)} %get-tuple-element.37), channel_id=1, source_target_pairs={{2,0},{4,2},{6,4},{8,6},{10,8},{12,10},{14,12},{3,1},{5,3},{7,5},{... | collective-permute-start | bytes 1032200 | tf_op jit(solution)/shard_map/ppermute | solution.py:481
  11.4 2.3 %collective-permute-start.2 = (f32[312,128]{1,0:T(8,128)S(1)}, f32[312,128]{1,0:T(8,128)S(1)}, u32[]{:S(2)}, u32[]{:S(2)}) collective-permute-start(f32[312,128]{1,0:T(8,128)S(1)} %get-tuple-element.38.own), channel_id=1, source_target_pairs={{0,1},{1,0},{2,3},{3,2},{4,5},{5,4},{6,7},{7,6},{8,9},{9,8},{10,11... | collective-permute-start | bytes 479240 | tf_op jit(solution)/shard_map/ppermute | solution.py:484
  13.9 19.9 %collective-permute-start.3 = (f32[2,208,128]{2,1,0:T(8,128)S(1)}, f32[2,208,128]{2,1,0:T(8,128)S(1)}, u32[]{:S(2)}, u32[]{:S(2)}) collective-permute-start(f32[2,208,128]{2,1,0:T(8,128)S(1)} %get-tuple-element.42), channel_id=1, source_target_pairs={{0,2},{2,4},{4,6},{6,8},{8,10},{10,12},{12,14},{1,3},{3,5},{5,7},{... | collective-permute-start | bytes 638984 | tf_op jit(solution)/shard_map/ppermute | solution.py:480
  16.1 17.7 %collective-permute-start.4 = (f32[2,208,128]{2,1,0:T(8,128)S(1)}, f32[2,208,128]{2,1,0:T(8,128)S(1)}, u32[]{:S(2)}, u32[]{:S(2)}) collective-permute-start(f32[2,208,128]{2,1,0:T(8,128)S(1)} %get-tuple-element.43), channel_id=1, source_target_pairs={{2,0},{4,2},{6,4},{8,6},{10,8},{12,10},{14,12},{3,1},{5,3},{7,5},{... | collective-permute-start | bytes 638984 | tf_op jit(solution)/shard_map/ppermute | solution.py:481
  27.6 21.7 %collective-permute-start.7 = (f32[2,320,128]{2,1,0:T(8,128)S(1)}, f32[2,320,128]{2,1,0:T(8,128)S(1)}, u32[]{:S(2)}, u32[]{:S(2)}) collective-permute-start(f32[2,320,128]{2,1,0:T(8,128)S(1)} %get-tuple-element.49), channel_id=1, source_target_pairs={{0,2},{2,4},{4,6},{6,8},{8,10},{10,12},{12,14},{1,3},{3,5},{5,7},{... | collective-permute-start | bytes 983048 | tf_op jit(solution)/shard_map/ppermute | solution.py:480
  29.5 21.0 %collective-permute-start.8 = (f32[2,320,128]{2,1,0:T(8,128)S(1)}, f32[2,320,128]{2,1,0:T(8,128)S(1)}, u32[]{:S(2)}, u32[]{:S(2)}) collective-permute-start(f32[2,320,128]{2,1,0:T(8,128)S(1)} %get-tuple-element.51), channel_id=1, source_target_pairs={{2,0},{4,2},{6,4},{8,6},{10,8},{12,10},{14,12},{3,1},{5,3},{7,5},{... | collective-permute-start | bytes 983048 | tf_op jit(solution)/shard_map/ppermute | solution.py:481
  39.9 16.3 %collective-permute-start.5 = (f32[2,160,128]{2,1,0:T(8,128)S(1)}, f32[2,160,128]{2,1,0:T(8,128)S(1)}, u32[]{:S(2)}, u32[]{:S(2)}) collective-permute-start(f32[2,160,128]{2,1,0:T(8,128)S(1)} %get-tuple-element.45), channel_id=1, source_target_pairs={{0,2},{2,4},{4,6},{6,8},{8,10},{10,12},{12,14},{1,3},{3,5},{5,7},{... | collective-permute-start | bytes 491528 | tf_op jit(solution)/shard_map/ppermute | solution.py:480
  41.9 14.2 %collective-permute-start.6 = (f32[2,160,128]{2,1,0:T(8,128)S(1)}, f32[2,160,128]{2,1,0:T(8,128)S(1)}, u32[]{:S(2)}, u32[]{:S(2)}) collective-permute-start(f32[2,160,128]{2,1,0:T(8,128)S(1)} %get-tuple-element.47), channel_id=1, source_target_pairs={{2,0},{4,2},{6,4},{8,6},{10,8},{12,10},{14,12},{3,1},{5,3},{7,5},{... | collective-permute-start | bytes 491528 | tf_op jit(solution)/shard_map/ppermute | solution.py:481

commit v2 on v1

--- a/solution.py
+++ b/solution.py
@@ -1,3 +1,4 @@
+import functools
 import math
 
 import jax
@@ -91,6 +92,15 @@
     return packed
 
 
+def is_even(bins):
+    return lax.rem(lax.axis_index("region") * bins + lax.axis_index("bin"), 2) == 0
+
+
+def by_parity(even, run):
+    pl.when(even)(lambda: run(True))
+    pl.when(jnp.logical_not(even))(lambda: run(False))
+
+
 def split(value):
     return value[:, :LANES], value[:, LANES:]
 
@@ -104,19 +114,24 @@
             src[t, pl.ds(row, ROWS), :] = grown * inverse[t]
 
 
-def make_packs(src, base, local, up_ref, down_ref):
-    for ref, up in ((up_ref, True), (down_ref, False)):
-        for k, d0, count, row in segments(up):
-            j = ROWS - k if up else k - 1
-            for t in range(TILES):
-                ref[t, pl.ds(local * PACK + row, count), :] = src[t, pl.ds(base + d0 * ROWS + j, count, stride=ROWS), :]
+def make_packs(even, src, base, local, near, far):
+    def run(north_near):
+        for ref, up in ((near, north_near), (far, not north_near)):
+            for k, d0, count, row in segments(up):
+                j = ROWS - k if up else k - 1
+                for t in range(TILES):
+                    value = src[t, pl.ds(base + d0 * ROWS + j, count, stride=ROWS), :]
+                    ref[t, pl.ds(local * PACK + row, count), :] = value
+
+    by_parity(even, run)
 
 
 def head_kernel(
-    spec, u_hbm, v_hbm, mask_hbm, depth_hbm, sx_hbm, sy_hbm,
-    raw, src0, push, damp_ref, geo, up_ref, down_ref,
+    bins, spec, u_hbm, v_hbm, mask_hbm, depth_hbm, sx_hbm, sy_hbm,
+    raw, src0, push, damp_ref, geo, near, far,
     u_ref, v_ref, mask_ref, depth_ref, sx_ref, sy_ref, small_sem, in_sem,
 ):
+    even = is_even(bins)
     off = pl.multiple_of(lax.axis_index("bin") * ROWS, ROWS)
     own = pl.ds(off, ROWS)
     small = [
@@ -156,9 +171,9 @@
             geo[g, t] = tile
         rows = slice(tail + g * SUB, tail + (g + 1) * SUB)
         for t, tile in enumerate(split(fields[g])):
-            up_ref[t, rows, :] = tile[ROWS - SUB :, :]
-            down_ref[t, rows, :] = tile[:SUB, :]
-    for ref in (up_ref, down_ref):
+            near[t, rows, :] = jnp.where(even, tile[ROWS - SUB :, :], tile[:SUB, :])
+            far[t, rows, :] = jnp.where(even, tile[:SUB, :], tile[ROWS - SUB :, :])
+    for ref in (near, far):
         for t in range(TILES):
             ref[t, tail + 3 * SUB :, :] = jnp.zeros((GEO - 3 * SUB, LANES), jnp.float32)
     for t, tile in enumerate(split(mask)):
@@ -191,16 +206,17 @@
         inverse = [geo[3, t] / (1.0 + of_freq(SIGMA, f) * damps[t]) for t in range(TILES)]
         base = pl.multiple_of(f * SPAN, SPAN)
         make_sources(raw, src0, push, inverse, f, base)
-        make_packs(src0, base, f, up_ref, down_ref)
+        make_packs(even, src0, base, f, near, far)
         return carry
 
     lax.fori_loop(0, CHUNKS[0], body, 0)
 
 
-def rest_kernel(raw, src0, push, damp, geo, *refs):
+def rest_kernel(bins, raw, src0, push, damp, geo, *refs):
     n = len(CHUNKS) - 1
     src, edge = refs[:2]
-    ups, downs = refs[2 : 2 + n], refs[2 + n :]
+    nears, fars = refs[2 : 2 + n], refs[2 + n :]
+    even = is_even(bins)
     at = CHUNKS[0]
     for c in range(n):
         def body(local, carry, c=c, at=at):
@@ -208,7 +224,7 @@
             inverse = [geo[3, t] / (1.0 + of_freq(SIGMA, f) * damp[t]) for t in range(TILES)]
             base = pl.multiple_of((f - CHUNKS[0]) * SPAN, SPAN)
             make_sources(raw, src, push, inverse, f, base)
-            make_packs(src, base, local, ups[c], downs[c])
+            make_packs(even, src, base, local, nears[c], fars[c])
             return carry
 
         lax.fori_loop(0, CHUNKS[c + 1], body, 0)
@@ -228,13 +244,12 @@
         edge[(DIRS + g) * ROWS : (DIRS + g + 1) * ROWS, :] = put_edges([(geo[g, 0], geo[g, 1])] * F)
 
 
-def join_kernel(own, other, up_in, down_in, edge, up_out, down_out, tails, sem):
+def join_kernel(bins, own, other, near_in, far_in, edge, near, far, tails, sem):
     lanes = own_lanes()
     for d in range(EDGES):
         rows = slice(d * ROWS, (d + 1) * ROWS)
         edge[rows, :] = jnp.where(lanes, own[rows, :], other[rows, :])
-    copies = []
-    for i, (out, up) in enumerate(((up_out, True), (down_out, False))):
+    for i, up in enumerate((True, False)):
         pieces = [
             (row, count, pl.ds(d0 * ROWS + (ROWS - k if up else k - 1), count, stride=ROWS))
             for k, d0, count, row in segments(up)
@@ -250,15 +265,21 @@
                 at += size
         rest = 2 * TAIL - PACK - 3 * SUB
         tails[i, 1, TAIL - rest :, :] = jnp.zeros((rest, LANES), jnp.float32)
-        copies.append(
+
+    def run(north_near):
+        copies = [
             pltpu.make_async_copy(tails.at[i], out.at[:, pl.ds(CHUNKS[1] * PACK, TAIL)], sem.at[i])
-        )
-        copies[-1].start()
-    for copy in copies:
-        copy.wait()
-
-
-def border_kernel(own, up, down, field):
+            for i, out in enumerate((near, far) if north_near else (far, near))
+        ]
+        for copy in copies:
+            copy.start()
+        for copy in copies:
+            copy.wait()
+
+    by_parity(is_even(bins), run)
+
+
+def border_kernel(bins, own, near, far, field):
     zero = jnp.zeros((ROWS, LANES), jnp.float32)
     for s in range(SUB):
         field[s, :PAD, :] = zero
@@ -272,8 +293,10 @@
     tail = CHUNKS[1] * PACK
     halves = [
         jnp.concatenate([ref[0, tail : tail + TAIL, :], ref[1, tail : tail + TAIL, :]], axis=0)
-        for ref in (up, down)
+        for ref in (near, far)
     ]
+    even = is_even(bins)
+    halves = [jnp.where(even, halves[1], halves[0]), jnp.where(even, halves[0], halves[1])]
     for value, is_up in zip(halves, (True, False)):
         for k, d0, count, row in segments(is_up):
             place = PAD + d0 * PITCH + (SUB - k if is_up else SUB + ROWS + k - 1)
@@ -310,18 +333,30 @@
                 field[step + 1, row : row + ROWS, :] = now + moved
 
 
-def step_kernel(first, start, count, source_at, *refs):
-    if first:
-        src, up, down, border, geo_own, out, geo, field_a, field_b, turn, done, sem = refs
-        tail = count * PACK
+def tables_kernel(bins, near, far, geo_own, depth, turn):
+    even = is_even(bins)
+    tail = CHUNKS[0] * PACK
+    for t in range(TILES):
+        whole = []
         for g in range(3):
             rows = slice(tail + g * SUB, tail + (g + 1) * SUB)
-            for t in range(TILES):
-                geo[g, t, :SUB] = up[t, rows, :]
-                geo[g, t, SUB : SUB + ROWS] = geo_own[g, t]
-                geo[g, t, SUB + ROWS :] = down[t, rows, :]
+            south = jnp.where(even, far[t, rows, :], near[t, rows, :])
+            north = jnp.where(even, near[t, rows, :], far[t, rows, :])
+            own = geo_own[g, t]
+            whole.append([jnp.concatenate([south, own[:SUB]], axis=0), jnp.concatenate([own[SUB:], north], axis=0)])
+        for half in range(2):
+            depth[t, half * ROWS : (half + 1) * ROWS, :] = whole[0][half]
+            sx, sy = 0.5 * whole[1][half], 0.5 * whole[2][half]
+            for d in range(DIRS):
+                turn[t, d * PITCH + half * ROWS : d * PITCH + (half + 1) * ROWS, :] = SIN[d] * sx - COS[d] * sy
+
+
+def step_kernel(bins, first, start, count, source_at, *refs):
+    even = is_even(bins)
+    if first:
+        src, near, far, border, geo, turn, out, field_a, field_b, done, sem = refs
     else:
-        src, up, down, border, geo, _, out, field_a, field_b, turn, done, sem = refs
+        src, near, far, border, geo, turn, _, out, field_a, field_b, done, sem = refs
     zero = jnp.zeros((ROWS, LANES), jnp.float32)
     for t in range(TILES):
         for field in (field_a, field_b):
@@ -330,11 +365,6 @@
         for d in range(DIRS + 1):
             row = PAD + d * PITCH - SUB
             field_a[t, row : row + 2 * SUB, :] = zero
-        for half in range(2):
-            rows = slice(half * ROWS, (half + 1) * ROWS)
-            sx, sy = 0.5 * geo[1, t, rows], 0.5 * geo[2, t, rows]
-            for d in range(DIRS):
-                turn[t, d * PITCH + half * ROWS : d * PITCH + (half + 1) * ROWS, :] = SIN[d] * sx - COS[d] * sy
     lanes = lane_iota()
     at_first, at_last = lanes == 0, lanes == LANES - 1
     quarter = DIRS // 4
@@ -353,12 +383,15 @@
             row = PAD + d * PITCH + SUB
             for t in range(TILES):
                 field_a[t, row : row + ROWS, :] = src[t, pl.ds(base + d * ROWS, ROWS), :]
-        for ref, is_up in ((up, True), (down, False)):
-            for k, d0, number, row in segments(is_up):
-                place = PAD + d0 * PITCH + (SUB - k if is_up else SUB + ROWS + k - 1)
-                place = pl.ds(place, number, stride=PITCH)
-                for t in range(TILES):
-                    field_a[t, place, :] = ref[t, pl.ds(i * PACK + row, number), :]
+        def unpack(north_near):
+            for ref, is_up in ((near, not north_near), (far, north_near)):
+                for k, d0, number, row in segments(is_up):
+                    place = PAD + d0 * PITCH + (SUB - k if is_up else SUB + ROWS + k - 1)
+                    place = pl.ds(place, number, stride=PITCH)
+                    for t in range(TILES):
+                        field_a[t, place, :] = ref[t, pl.ds(i * PACK + row, number), :]
+
+        by_parity(even, unpack)
 
         freq = start + i
         speed = of_freq(SPEED, freq)
@@ -373,7 +406,7 @@
         def advance(step, old, new):
             last = step == SUB - 1
             for part in (SUB,) if last else (0, ROWS):
-                depth = [speed * geo[0, t, part : part + ROWS] for t in range(TILES)]
+                depth = [speed * geo[t, part : part + ROWS, :] for t in range(TILES)]
 
                 def load(d, shift=0):
                     row = PAD + (d % DIRS) * PITCH + part + shift
@@ -396,7 +429,12 @@
                             up_x = jnp.where(at_last, rolled[t + 1] if t < TILES - 1 else outer, rolled[t])
                         vt = turn[t, d * PITCH + part : d * PITCH + part + ROWS, :]
                         up_t = jnp.where(vt > 0.0, before[t], after[t])
-                        moved = depth[t] * (cos * up_x + sin * up_y[t] - (cos + sin) * now[t])
+                        if sin == 0.0:
+                            moved = depth[t] * (up_x - now[t])
+                        elif cos == 0.0:
+                            moved = depth[t] * (up_y[t] - now[t])
+                        else:
+                            moved = depth[t] * (cos * up_x + sin * up_y[t] - (cos + sin) * now[t])
                         value = now[t] + (moved + speed * jnp.abs(vt) * (up_t - now[t]))
                         if last:
                             done[lax.rem(i, 2), d, :, t * LANES : (t + 1) * LANES] = value
@@ -437,8 +475,9 @@
         pltpu.with_memory_space_constraint(x, pltpu.HBM)
         for x in (spectrum, wind_u, wind_v, sea_mask, depth_factor, slope_x, slope_y)
     ]
-    raw, src0, push, damp, geo_own, up0, down0 = pl.pallas_call(
-        head_kernel,
+    bins = lax.axis_size("bin")
+    raw, src0, push, damp, geo_own, near0, far0 = pl.pallas_call(
+        functools.partial(head_kernel, bins),
         out_shape=[
             shape(TILES, nbins, *tile),
             shape(TILES, CHUNKS[0] * SPAN, LANES),
@@ -459,7 +498,7 @@
 
     n = len(CHUNKS) - 1
     outs = pl.pallas_call(
-        rest_kernel,
+        functools.partial(rest_kernel, bins),
         out_shape=[
             shape(TILES, (F - CHUNKS[0]) * SPAN, LANES),
             shape(EDGES * rows, LANES),
@@ -472,18 +511,27 @@
         name="rest",
     )(raw, src0, push, damp, geo_own)
     src, edge = outs[:2]
-    ups, downs = [up0, *outs[2 : 2 + n]], [down0, *outs[2 + n :]]
-
-    blocks = lax.axis_size("region") * lax.axis_size("bin")
-    up_pairs = [(i, i + 1) for i in range(blocks - 1)]
-    down_pairs = [(j, i) for i, j in up_pairs]
-    send_up = lambda x: lax.ppermute(x, ("region", "bin"), up_pairs)
-    send_down = lambda x: lax.ppermute(x, ("region", "bin"), down_pairs)
-
-    from_south, from_north = [send_up(ups[0])], [send_down(downs[0])]
+    nears, fars = [near0, *outs[2 : 2 + n]], [far0, *outs[2 + n :]]
+
+    blocks = lax.axis_size("region") * bins
+
+    def exchange(value, odd):
+        pairs = [(i, i + 1) for i in range(odd, blocks - 1, 2)]
+        return lax.ppermute(value, ("region", "bin"), pairs + [(j, i) for i, j in pairs])
+
+    from_near, from_far = [exchange(nears[0], 0)], [exchange(fars[0], 1)]
+    depth, turn = pl.pallas_call(
+        functools.partial(tables_kernel, bins),
+        out_shape=[shape(TILES, PITCH, LANES), shape(TILES, DIRS * PITCH, LANES)],
+        in_specs=[VMEM] * 3,
+        out_specs=[VMEM] * 2,
+        compiler_params=params,
+        cost_estimate=pl.CostEstimate(flops=100_000_000_000, bytes_accessed=1000, transcendentals=0),
+        name="tables",
+    )(from_near[0], from_far[0], geo_own)
     other = lax.ppermute(edge, "pt", [(0, 1), (1, 0)])
-    edge, ups[1], downs[1] = pl.pallas_call(
-        join_kernel,
+    edge, nears[1], fars[1] = pl.pallas_call(
+        functools.partial(join_kernel, bins),
         out_shape=[shape(EDGES * rows, LANES), shape(TILES, heights[1], LANES), shape(TILES, heights[1], LANES)],
         in_specs=[VMEM, VMEM, ANY, ANY],
         out_specs=[VMEM, ANY, ANY],
@@ -492,38 +540,36 @@
         compiler_params=params,
         cost_estimate=cost,
         name="join",
-    )(edge, other, ups[1], downs[1])
-    wait = (from_south[0], from_north[0])
-    from_south += [send_up(ups[1]), send_up(after(ups[2], *wait))]
-    from_north += [send_down(downs[1]), send_down(after(downs[2], *wait))]
+    )(edge, other, nears[1], fars[1])
+    from_near += [exchange(nears[1], 0), exchange(after(nears[2], depth), 0)]
+    from_far.append(exchange(fars[1], 1))
     border = pl.pallas_call(
-        border_kernel,
+        functools.partial(border_kernel, bins),
         out_shape=shape(SUB, HEIGHT, LANES),
         in_specs=[VMEM] * 3,
         out_specs=VMEM,
         compiler_params=params,
         cost_estimate=cost,
         name="border",
-    )(edge, from_south[1], from_north[1])
-
-
-    start, geo, result = 0, None, None
+    )(edge, from_near[1], from_far[1])
+
+
+    from_far.append(exchange(after(fars[2], border), 1))
+
+    start, result = 0, None
     for c, count in enumerate(CHUNKS):
         first = c == 0
-        operands = [src0 if first else src, from_south[c], from_north[c], border]
-        in_specs = [VMEM] * 5
+        operands = [src0 if first else src, from_near[c], from_far[c], border, depth, turn]
+        in_specs = [VMEM] * 6
         out_shape = [shape(nbins, rows, cols)]
         aliases = {}
-        if first:
-            operands.append(geo_own)
-            out_shape.append(shape(3, TILES, PITCH, LANES))
-        else:
-            operands += [geo, result]
+        if not first:
+            operands.append(result)
             in_specs.append(ANY)
             aliases = {len(operands) - 1: 0}
 
         def kernel(*refs, first=first, start=start, count=count):
-            step_kernel(first, start, count, start - (0 if first else CHUNKS[0]), *refs)
+            step_kernel(bins, first, start, count, start - (0 if first else CHUNKS[0]), *refs)
 
         outs = pl.pallas_call(
             kernel,
@@ -531,7 +577,7 @@
             in_specs=in_specs,
             out_specs=[ANY, VMEM][: len(out_shape)],
             scratch_shapes=[scratch(TILES, HEIGHT, LANES)] * 2
-            + [scratch(TILES, DIRS * PITCH, LANES), scratch(2, DIRS, rows, cols), pltpu.SemaphoreType.DMA((2, 4))],
+            + [scratch(2, DIRS, rows, cols), pltpu.SemaphoreType.DMA((2, 4))],
             input_output_aliases=aliases,
             compiler_params=params,
             cost_estimate=cost,
@@ -539,10 +585,10 @@
         )(*operands)
         result = outs[0]
         if first:
-            geo = outs[1]
             for later in range(3, len(CHUNKS)):
-                from_south.append(send_up(after(ups[later], geo)))
-                from_north.append(send_down(after(downs[later], geo)))
+                value, other, result = lax.optimization_barrier((nears[later], fars[later], result))
+                from_near.append(exchange(value, 0))
+                from_far.append(exchange(other, 1))
         start += count
     return result
 

time: 59.7 us -> 56.8 us (0.951)
  the two profiles are of different devices: /device:TPU:9 before, /device:TPU:2 now
where the time goes in v2:
time: 56.8 us; the launch traced here: 56.6 us
  Pallas kernels  23.2 us (41%)
  starting transfers between devices  18.6 us (33%)
  waiting for transfers between devices  14.7 us (26%)
    ppermute x8, starting transfers between devices, exchange(): lax.ppermute(value, ('region', 'bin'), pairs + [(j, i) for i, j in pairs])  18.5 us
    pallas_call x4, Pallas kernels, per_device(): pl.pallas_call(kernel, out_shape=out_shape, in_specs=in_specs, out_specs=...  17.2 us
    ppermute x8, waiting for transfers between devices, exchange(): lax.ppermute(value, ('region', 'bin'), pairs + [(j, i) for i, j in pairs])  13.3 us
    pallas_call x1, Pallas kernels, per_device(): pl.pallas_call(functools.partial(head_kernel, bins), out_shape=[shape(TIL...  2.9 us
    pallas_call x1, Pallas kernels, per_device(): pl.pallas_call(functools.partial(rest_kernel, bins), out_shape=[shape(TIL...  2.45 us
    ppermute x1, waiting for transfers between devices, per_device(): other = lax.ppermute(edge, 'pt', [(0, 1), (1, 0)])  1.38 us
  transfers between devices with their start and end apart: 9, of which 3 were waited for; matrix products, arithmetic and copies ran while one was open for 0% of the time, Pallas kernels for 30%

profile of v2, /device:TPU:2, one launch (start us, length us, event | category | flops | bytes accessed | tf_op | source)
XLA Modules:
  0.0 56.6 jit_solution(10771109456606669346)
XLA Ops:
  0.0 2.9 %head.1 = (f32[2,432,8,128]{3,2,1,0:T(8,128)S(1)}, f32[2,1152,128]{2,1,0:T(8,128)S(1)}, f32[2,36,8,128]{3,2,1,0:T(8,128)S(1)}, f32[2,8,128]{2,1,0:T(8,128)S(1)},...) custom-call(f32[432,8,256]{2,1,0:T(8,128)} %spec.1, f32[8,256]{1,0:T(8,128)} %u_hbm.1, ...), custom_call_target="tpu_custom_call" | custom-call | flops 1000 | bytes 1000 | tf_op jit(solution)/shard_map/head/pallas_call | solution.py:479
  2.9 0.1 collective-permute-start
  3.0 4.9 %collective-permute-start.1 = (f32[2,336,128]{2,1,0:T(8,128)S(1)}, f32[2,336,128]{2,1,0:T(8,128)S(1)}, u32[]{:S(2)}, u32[]{:S(2)}) collective-permute-start(f32[2,336,128]{2,1,0:T(8,128)S(1)} %get-tuple-element.39), channel_id=1, source_target_pairs={{2,4},{6,8},{10,12},{4,2},{8,6},{12,10},{3,5},{7,9},{11,13},{5,3},... | collective-permute-start | bytes 1032200 | tf_op jit(solution)/shard_map/ppermute | solution.py:520
  7.9 2.5 %rest.1 = (f32[2,2304,128]{2,1,0:T(8,128)S(1)}, f32[312,128]{1,0:T(8,128)S(1)}, f32[2,208,128]{2,1,0:T(8,128)S(1)}, f32[2,320,128]{2,1,0:T(8,128)S(1)}, f32[2,16...) custom-call(f32[2,432,8,128]{3,2,1,0:T(8,128)S(1)} %get-tuple-element., ...), custom_call_target="tpu_custom_call" | custom-call | flops 1000 | bytes 1000 | tf_op jit(solution)/shard_map/rest/pallas_call | solution.py:500
  10.4 0.1 collective-permute-start.2
  10.4 1.4 %collective-permute-done.2.other = f32[312,128]{1,0:T(8,128)S(1)} collective-permute-done((f32[312,128]{1,0:T(8,128)S(1)}, f32[312,128]{1,0:T(8,128)S(1)}, u32[]{:S(2)}, u32[]{:S(2)}) %collective-permute-start.2) | collective-permute-done | bytes 159776 | tf_op jit(solution)/shard_map/ppermute | solution.py:532
  11.8 0.1 join.1
  12.0 0.1 collective-permute-start.3
  12.0 4.9 %collective-permute-start.4 = (f32[2,208,128]{2,1,0:T(8,128)S(1)}, f32[2,208,128]{2,1,0:T(8,128)S(1)}, u32[]{:S(2)}, u32[]{:S(2)}) collective-permute-start(f32[2,208,128]{2,1,0:T(8,128)S(1)} %get-tuple-element.45), channel_id=1, source_target_pairs={{2,4},{6,8},{10,12},{4,2},{8,6},{12,10},{3,5},{7,9},{11,13},{5,3},... | collective-permute-start | bytes 638984 | tf_op jit(solution)/shard_map/ppermute | solution.py:520
  17.0 8.9 %collective-permute-done.near.refs_1_ = f32[2,336,128]{2,1,0:T(8,128)S(1)} collective-permute-done((f32[2,336,128]{2,1,0:T(8,128)S(1)}, f32[2,336,128]{2,1,0:T(8,128)S(1)}, u32[]{:S(2)}, u32[]{:S(2)}) %collective-permute-start) | collective-permute-done | bytes 344096 | tf_op jit(solution)/shard_map/ppermute | solution.py:520
  25.9 0.0 collective-permute-done.1.far.refs_2_
  25.9 0.1 tables.1
  25.9 0.1 collective-permute-start.7
  26.0 4.4 %collective-permute-done.3.near.refs_1_ = f32[2,208,128]{2,1,0:T(8,128)S(1)} collective-permute-done((f32[2,208,128]{2,1,0:T(8,128)S(1)}, f32[2,208,128]{2,1,0:T(8,128)S(1)}, u32[]{:S(2)}, u32[]{:S(2)}) %collective-permute-start.3) | collective-permute-done | bytes 213024 | tf_op jit(solution)/shard_map/ppermute | solution.py:520
  30.4 0.0 collective-permute-done.4.far.refs_2_
  30.4 0.5 border.1.refs_3_
  30.9 3.5 %collective-permute-start.8 = (f32[2,320,128]{2,1,0:T(8,128)S(1)}, f32[2,320,128]{2,1,0:T(8,128)S(1)}, u32[]{:S(2)}, u32[]{:S(2)}) collective-permute-start(f32[2,320,128]{2,1,0:T(8,128)S(1)} %get-tuple-element.53), channel_id=1, source_target_pairs={{2,4},{6,8},{10,12},{4,2},{8,6},{12,10},{3,5},{7,9},{11,13},{5,3},... | collective-permute-start | bytes 983048 | tf_op jit(solution)/shard_map/ppermute | solution.py:520
  34.4 5.5 %steps_0.1.refs_6_ = f32[432,8,256]{2,1,0:T(8,128)} custom-call(f32[2,1152,128]{2,1,0:T(8,128)S(1)} %get-tuple-element.31.src0.refs_0_, f32[2,336,128]{2,1,0:T(8,128)S(1)} %collective-permute-done.near.refs_1_, f32[2,336,128]{2,1,0:T(8,128)S(1)} %collective-permute-done.1.far.refs_2_, f32[4,592,128]{2,1,0:T(8,128)S(1)} %border.1.refs_3_, ...), custom_call_target="tpu_custom_call" | custom-call | flops 1000 | bytes 1000 | tf_op jit(solution)/shard_map/steps_0/pallas_call | solution.py:574
  39.8 0.1 collective-permute-start.5
  39.9 4.9 %collective-permute-start.6 = (f32[2,160,128]{2,1,0:T(8,128)S(1)}, f32[2,160,128]{2,1,0:T(8,128)S(1)}, u32[]{:S(2)}, u32[]{:S(2)}) collective-permute-start(f32[2,160,128]{2,1,0:T(8,128)S(1)} %get-tuple-element.49), channel_id=1, source_target_pairs={{2,4},{6,8},{10,12},{4,2},{8,6},{12,10},{3,5},{7,9},{11,13},{5,3},... | collective-permute-start | bytes 491528 | tf_op jit(solution)/shard_map/ppermute | solution.py:520
  44.9 3.1 %steps_1.1.refs_6_ = f32[432,8,256]{2,1,0:T(8,128)} custom-call(f32[2,2304,128]{2,1,0:T(8,128)S(1)} %get-tuple-element.35.refs_0_, f32[2,208,128]{2,1,0:T(8,128)S(1)} %collective-permute-done.3.near.refs_1_, f32[2,208,128]{2,1,0:T(8,128)S(1)} %collective-permute-done.4.far.refs_2_, ...), custom_call_target="tpu_custom_call", output_to_operand_aliasing={{}: (6, {})} | custom-call | flops 1000 | bytes 1000 | tf_op jit(solution)/shard_map/steps_1/pallas_call | solution.py:574
  48.0 0.0 collective-permute-done.7.refs_1_
  48.0 0.0 collective-permute-done.8.refs_2_
  48.0 5.5 %steps_2.1.refs_6_ = f32[432,8,256]{2,1,0:T(8,128)} custom-call(f32[2,2304,128]{2,1,0:T(8,128)S(1)} %get-tuple-element.35.refs_0_, f32[2,320,128]{2,1,0:T(8,128)S(1)} %collective-permute-done.7.refs_1_, f32[2,320,128]{2,1,0:T(8,128)S(1)} %collective-permute-done.8.refs_2_, f32[4,592,128]{2,1,0:T(8,128)S(1)} %border.1.refs_3_, ...), custom_call_target="tpu_custom_call", output_to_operand_aliasing={{}: (6, {})} | custom-call | flops 1000 | bytes 1000 | tf_op jit(solution)/shard_map/steps_2/pallas_call | solution.py:574
  53.5 0.0 collective-permute-done.5.refs_1_
  53.5 0.0 collective-permute-done.6.refs_2_
  53.5 3.1 %steps_3.1 = f32[432,8,256]{2,1,0:T(8,128)} custom-call(f32[2,2304,128]{2,1,0:T(8,128)S(1)} %get-tuple-element.35.refs_0_, f32[2,160,128]{2,1,0:T(8,128)S(1)} %collective-permute-done.5.refs_1_, f32[2,160,128]{2,1,0:T(8,128)S(1)} %collective-permute-done.6.refs_2_, f32[4,592,128]{2,1,0:T(8,128)S(1)} %border.1.refs_3_, ...), custom_call_target="tpu_custom_call", output_to_operand_aliasing={{}: (6, {})} | custom-call | flops 1000 | bytes 1000 | tf_op jit(solution)/shard_map/steps_3/pallas_call | solution.py:574
Async XLA Ops:
  2.9 23.0 %collective-permute-start = (f32[2,336,128]{2,1,0:T(8,128)S(1)}, f32[2,336,128]{2,1,0:T(8,128)S(1)}, u32[]{:S(2)}, u32[]{:S(2)}) collective-permute-start(f32[2,336,128]{2,1,0:T(8,128)S(1)} %get-tuple-element.38), channel_id=1, source_target_pairs={{0,2},{4,6},{8,10},{12,14},{2,0},{6,4},{10,8},{14,12},{1,3},{5,7},... | collective-permute-start | bytes 1032200 | tf_op jit(solution)/shard_map/ppermute | solution.py:520
  3.0 22.9 %collective-permute-start.1 = (f32[2,336,128]{2,1,0:T(8,128)S(1)}, f32[2,336,128]{2,1,0:T(8,128)S(1)}, u32[]{:S(2)}, u32[]{:S(2)}) collective-permute-start(f32[2,336,128]{2,1,0:T(8,128)S(1)} %get-tuple-element.39), channel_id=1, source_target_pairs={{2,4},{6,8},{10,12},{4,2},{8,6},{12,10},{3,5},{7,9},{11,13},{5,3},... | collective-permute-start | bytes 1032200 | tf_op jit(solution)/shard_map/ppermute | solution.py:520
  10.4 1.5 %collective-permute-start.2 = (f32[312,128]{1,0:T(8,128)S(1)}, f32[312,128]{1,0:T(8,128)S(1)}, u32[]{:S(2)}, u32[]{:S(2)}) collective-permute-start(f32[312,128]{1,0:T(8,128)S(1)} %get-tuple-element.40.own), channel_id=1, source_target_pairs={{0,1},{1,0},{2,3},{3,2},{4,5},{5,4},{6,7},{7,6},{8,9},{9,8},{10,11... | collective-permute-start | bytes 479240 | tf_op jit(solution)/shard_map/ppermute | solution.py:532
  12.0 18.5 %collective-permute-start.3 = (f32[2,208,128]{2,1,0:T(8,128)S(1)}, f32[2,208,128]{2,1,0:T(8,128)S(1)}, u32[]{:S(2)}, u32[]{:S(2)}) collective-permute-start(f32[2,208,128]{2,1,0:T(8,128)S(1)} %get-tuple-element.44), channel_id=1, source_target_pairs={{0,2},{4,6},{8,10},{12,14},{2,0},{6,4},{10,8},{14,12},{1,3},{5,7},... | collective-permute-start | bytes 638984 | tf_op jit(solution)/shard_map/ppermute | solution.py:520
  12.0 18.4 %collective-permute-start.4 = (f32[2,208,128]{2,1,0:T(8,128)S(1)}, f32[2,208,128]{2,1,0:T(8,128)S(1)}, u32[]{:S(2)}, u32[]{:S(2)}) collective-permute-start(f32[2,208,128]{2,1,0:T(8,128)S(1)} %get-tuple-element.45), channel_id=1, source_target_pairs={{2,4},{6,8},{10,12},{4,2},{8,6},{12,10},{3,5},{7,9},{11,13},{5,3},... | collective-permute-start | bytes 638984 | tf_op jit(solution)/shard_map/ppermute | solution.py:520
  25.9 22.0 %collective-permute-start.7 = (f32[2,320,128]{2,1,0:T(8,128)S(1)}, f32[2,320,128]{2,1,0:T(8,128)S(1)}, u32[]{:S(2)}, u32[]{:S(2)}) collective-permute-start(f32[2,320,128]{2,1,0:T(8,128)S(1)} %get-tuple-element.51), channel_id=1, source_target_pairs={{0,2},{4,6},{8,10},{12,14},{2,0},{6,4},{10,8},{14,12},{1,3},{5,7},... | collective-permute-start | bytes 983048 | tf_op jit(solution)/shard_map/ppermute | solution.py:520
  30.9 17.1 %collective-permute-start.8 = (f32[2,320,128]{2,1,0:T(8,128)S(1)}, f32[2,320,128]{2,1,0:T(8,128)S(1)}, u32[]{:S(2)}, u32[]{:S(2)}) collective-permute-start(f32[2,320,128]{2,1,0:T(8,128)S(1)} %get-tuple-element.53), channel_id=1, source_target_pairs={{2,4},{6,8},{10,12},{4,2},{8,6},{12,10},{3,5},{7,9},{11,13},{5,3},... | collective-permute-start | bytes 983048 | tf_op jit(solution)/shard_map/ppermute | solution.py:520
  39.8 13.6 %collective-permute-start.5 = (f32[2,160,128]{2,1,0:T(8,128)S(1)}, f32[2,160,128]{2,1,0:T(8,128)S(1)}, u32[]{:S(2)}, u32[]{:S(2)}) collective-permute-start(f32[2,160,128]{2,1,0:T(8,128)S(1)} %get-tuple-element.48), channel_id=1, source_target_pairs={{0,2},{4,6},{8,10},{12,14},{2,0},{6,4},{10,8},{14,12},{1,3},{5,7},... | collective-permute-start | bytes 491528 | tf_op jit(solution)/shard_map/ppermute | solution.py:520
  39.9 13.6 %collective-permute-start.6 = (f32[2,160,128]{2,1,0:T(8,128)S(1)}, f32[2,160,128]{2,1,0:T(8,128)S(1)}, u32[]{:S(2)}, u32[]{:S(2)}) collective-permute-start(f32[2,160,128]{2,1,0:T(8,128)S(1)} %get-tuple-element.49), channel_id=1, source_target_pairs={{2,4},{6,8},{10,12},{4,2},{8,6},{12,10},{3,5},{7,9},{11,13},{5,3},... | collective-permute-start | bytes 491528 | tf_op jit(solution)/shard_map/ppermute | solution.py:520

commit v3 on v2

--- a/solution.py
+++ b/solution.py
@@ -19,7 +19,7 @@
 SENT = [HALF - 1 + 2 * (SUB - k) for k in range(1, SUB + 1)]
 PACK = sum(SENT)
 GEO = 16
-CHUNKS = (4, 2, 4, 2)
+CHUNKS = (3, 2, 4, 3)
 STRIP = 2 * SUB + 2
 EDGES = DIRS + 3
 TAIL = 48
@@ -554,7 +554,7 @@
     )(edge, from_near[1], from_far[1])
 
 
-    from_far.append(exchange(after(fars[2], border), 1))
+    from_far.append(exchange(after(fars[2], depth), 1))
 
     start, result = 0, None
     for c, count in enumerate(CHUNKS):

time: 56.8 us -> 56.1 us (0.988); the launches traced: 56.6 us -> 55.1 us
  waiting for transfers between devices: 14.7 us -> 13.2 us
    ppermute x8, waiting for transfers between devices: 13.3 us -> 11.8 us  [exchange(): lax.ppermute(value, ('region', 'bin'), pairs + [(j, i) for i, j in pairs])]
  transfers between devices with their start and end apart: 9 -> 9, of which waited for: 3 -> 3; matrix products, arithmetic and copies ran while one was open for 0% -> 0% of each run, Pallas kernels for 30% -> 29%
where the time goes in v3:
time: 56.1 us; the launch traced here: 55.1 us
  Pallas kernels  23.2 us (41%)
  starting transfers between devices  18.6 us (33%)
  waiting for transfers between devices  13.2 us (24%)
    ppermute x8, starting transfers between devices, exchange(): lax.ppermute(value, ('region', 'bin'), pairs + [(j, i) for i, j in pairs])  18.5 us
    pallas_call x4, Pallas kernels, per_device(): pl.pallas_call(kernel, out_shape=out_shape, in_specs=in_specs, out_specs=...  17.1 us
    ppermute x8, waiting for transfers between devices, exchange(): lax.ppermute(value, ('region', 'bin'), pairs + [(j, i) for i, j in pairs])  11.8 us
    pallas_call x1, Pallas kernels, per_device(): pl.pallas_call(functools.partial(head_kernel, bins), out_shape=[shape(TIL...  2.81 us
    pallas_call x1, Pallas kernels, per_device(): pl.pallas_call(functools.partial(rest_kernel, bins), out_shape=[shape(TIL...  2.55 us
    ppermute x1, waiting for transfers between devices, per_device(): other = lax.ppermute(edge, 'pt', [(0, 1), (1, 0)])  1.38 us
  transfers between devices with their start and end apart: 9, of which 3 were waited for; matrix products, arithmetic and copies ran while one was open for 0% of the time, Pallas kernels for 29%

profile of v3, /device:TPU:2, one launch (start us, length us, event | category | flops | bytes accessed | tf_op | source)
XLA Modules:
  0.0 55.1 jit_solution(13058128857387687867)
XLA Ops:
  0.0 2.8 %head.1 = (f32[2,432,8,128]{3,2,1,0:T(8,128)S(1)}, f32[2,864,128]{2,1,0:T(8,128)S(1)}, f32[2,36,8,128]{3,2,1,0:T(8,128)S(1)}, f32[2,8,128]{2,1,0:T(8,128)S(1)}, ...) custom-call(f32[432,8,256]{2,1,0:T(8,128)} %spec.1, f32[8,256]{1,0:T(8,128)} %u_hbm.1, ...), custom_call_target="tpu_custom_call" | custom-call | flops 1000 | bytes 1000 | tf_op jit(solution)/shard_map/head/pallas_call | solution.py:479
  2.8 0.1 collective-permute-start
  2.9 4.9 %collective-permute-start.1 = (f32[2,256,128]{2,1,0:T(8,128)S(1)}, f32[2,256,128]{2,1,0:T(8,128)S(1)}, u32[]{:S(2)}, u32[]{:S(2)}) collective-permute-start(f32[2,256,128]{2,1,0:T(8,128)S(1)} %get-tuple-element.39), channel_id=1, source_target_pairs={{2,4},{6,8},{10,12},{4,2},{8,6},{12,10},{3,5},{7,9},{11,13},{5,3},... | collective-permute-start | bytes 786440 | tf_op jit(solution)/shard_map/ppermute | solution.py:520
  7.8 2.6 %rest.1 = (f32[2,2592,128]{2,1,0:T(8,128)S(1)}, f32[312,128]{1,0:T(8,128)S(1)}, f32[2,208,128]{2,1,0:T(8,128)S(1)}, f32[2,320,128]{2,1,0:T(8,128)S(1)}, f32[2,24...) custom-call(f32[2,432,8,128]{3,2,1,0:T(8,128)S(1)} %get-tuple-element., ...), custom_call_target="tpu_custom_call" | custom-call | flops 1000 | bytes 1000 | tf_op jit(solution)/shard_map/rest/pallas_call | solution.py:500
  10.4 0.1 collective-permute-start.2
  10.5 1.4 %collective-permute-done.2.other = f32[312,128]{1,0:T(8,128)S(1)} collective-permute-done((f32[312,128]{1,0:T(8,128)S(1)}, f32[312,128]{1,0:T(8,128)S(1)}, u32[]{:S(2)}, u32[]{:S(2)}) %collective-permute-start.2) | collective-permute-done | bytes 159776 | tf_op jit(solution)/shard_map/ppermute | solution.py:532
  11.8 0.1 join.1
  12.0 0.1 collective-permute-start.3
  12.1 4.9 %collective-permute-start.4 = (f32[2,208,128]{2,1,0:T(8,128)S(1)}, f32[2,208,128]{2,1,0:T(8,128)S(1)}, u32[]{:S(2)}, u32[]{:S(2)}) collective-permute-start(f32[2,208,128]{2,1,0:T(8,128)S(1)} %get-tuple-element.45), channel_id=1, source_target_pairs={{2,4},{6,8},{10,12},{4,2},{8,6},{12,10},{3,5},{7,9},{11,13},{5,3},... | collective-permute-start | bytes 638984 | tf_op jit(solution)/shard_map/ppermute | solution.py:520
  17.0 0.7 %collective-permute-done.near.refs_1_ = f32[2,256,128]{2,1,0:T(8,128)S(1)} collective-permute-done((f32[2,256,128]{2,1,0:T(8,128)S(1)}, f32[2,256,128]{2,1,0:T(8,128)S(1)}, u32[]{:S(2)}, u32[]{:S(2)}) %collective-permute-start) | collective-permute-done | bytes 262176 | tf_op jit(solution)/shard_map/ppermute | solution.py:520
  17.7 0.0 collective-permute-done.1.far.refs_2_
  17.7 0.1 tables.1
  17.8 0.1 collective-permute-start.7
  17.9 4.9 %collective-permute-start.8 = (f32[2,320,128]{2,1,0:T(8,128)S(1)}, f32[2,320,128]{2,1,0:T(8,128)S(1)}, u32[]{:S(2)}, u32[]{:S(2)}) collective-permute-start(f32[2,320,128]{2,1,0:T(8,128)S(1)} %get-tuple-element.53), channel_id=1, source_target_pairs={{2,4},{6,8},{10,12},{4,2},{8,6},{12,10},{3,5},{7,9},{11,13},{5,3},... | collective-permute-start | bytes 983048 | tf_op jit(solution)/shard_map/ppermute | solution.py:520
  22.8 11.1 %collective-permute-done.3.near.refs_1_ = f32[2,208,128]{2,1,0:T(8,128)S(1)} collective-permute-done((f32[2,208,128]{2,1,0:T(8,128)S(1)}, f32[2,208,128]{2,1,0:T(8,128)S(1)}, u32[]{:S(2)}, u32[]{:S(2)}) %collective-permute-start.3) | collective-permute-done | bytes 213024 | tf_op jit(solution)/shard_map/ppermute | solution.py:520
  33.8 0.0 collective-permute-done.4.far.refs_2_
  33.9 0.5 border.1.refs_3_
  34.3 4.3 %steps_0.1.refs_6_ = f32[432,8,256]{2,1,0:T(8,128)} custom-call(f32[2,864,128]{2,1,0:T(8,128)S(1)} %get-tuple-element.31.src0.refs_0_, f32[2,256,128]{2,1,0:T(8,128)S(1)} %collective-permute-done.near.refs_1_, f32[2,256,128]{2,1,0:T(8,128)S(1)} %collective-permute-done.1.far.refs_2_, f32[4,592,128]{2,1,0:T(8,128)S(1)} %border.1.refs_3_, ...), custom_call_target="tpu_custom_call" | custom-call | flops 1000 | bytes 1000 | tf_op jit(solution)/shard_map/steps_0/pallas_call | solution.py:574
  38.6 0.1 collective-permute-start.5
  38.7 3.5 %collective-permute-start.6 = (f32[2,240,128]{2,1,0:T(8,128)S(1)}, f32[2,240,128]{2,1,0:T(8,128)S(1)}, u32[]{:S(2)}, u32[]{:S(2)}) collective-permute-start(f32[2,240,128]{2,1,0:T(8,128)S(1)} %get-tuple-element.49), channel_id=1, source_target_pairs={{2,4},{6,8},{10,12},{4,2},{8,6},{12,10},{3,5},{7,9},{11,13},{5,3},... | collective-permute-start | bytes 737288 | tf_op jit(solution)/shard_map/ppermute | solution.py:520
  42.2 3.1 %steps_1.1.refs_6_ = f32[432,8,256]{2,1,0:T(8,128)} custom-call(f32[2,2592,128]{2,1,0:T(8,128)S(1)} %get-tuple-element.35.refs_0_, f32[2,208,128]{2,1,0:T(8,128)S(1)} %collective-permute-done.3.near.refs_1_, f32[2,208,128]{2,1,0:T(8,128)S(1)} %collective-permute-done.4.far.refs_2_, ...), custom_call_target="tpu_custom_call", output_to_operand_aliasing={{}: (6, {})} | custom-call | flops 1000 | bytes 1000 | tf_op jit(solution)/shard_map/steps_1/pallas_call | solution.py:574
  45.3 0.0 collective-permute-done.7.refs_1_
  45.3 0.0 collective-permute-done.8.refs_2_
  45.3 5.5 %steps_2.1.refs_6_ = f32[432,8,256]{2,1,0:T(8,128)} custom-call(f32[2,2592,128]{2,1,0:T(8,128)S(1)} %get-tuple-element.35.refs_0_, f32[2,320,128]{2,1,0:T(8,128)S(1)} %collective-permute-done.7.refs_1_, f32[2,320,128]{2,1,0:T(8,128)S(1)} %collective-permute-done.8.refs_2_, f32[4,592,128]{2,1,0:T(8,128)S(1)} %border.1.refs_3_, ...), custom_call_target="tpu_custom_call", output_to_operand_aliasing={{}: (6, {})} | custom-call | flops 1000 | bytes 1000 | tf_op jit(solution)/shard_map/steps_2/pallas_call | solution.py:574
  50.8 0.0 collective-permute-done.5.refs_1_
  50.8 0.0 collective-permute-done.6.refs_2_
  50.8 4.3 %steps_3.1 = f32[432,8,256]{2,1,0:T(8,128)} custom-call(f32[2,2592,128]{2,1,0:T(8,128)S(1)} %get-tuple-element.35.refs_0_, f32[2,240,128]{2,1,0:T(8,128)S(1)} %collective-permute-done.5.refs_1_, f32[2,240,128]{2,1,0:T(8,128)S(1)} %collective-permute-done.6.refs_2_, f32[4,592,128]{2,1,0:T(8,128)S(1)} %border.1.refs_3_, ...), custom_call_target="tpu_custom_call", output_to_operand_aliasing={{}: (6, {})} | custom-call | flops 1000 | bytes 1000 | tf_op jit(solution)/shard_map/steps_3/pallas_call | solution.py:574
Async XLA Ops:
  2.8 14.9 %collective-permute-start = (f32[2,256,128]{2,1,0:T(8,128)S(1)}, f32[2,256,128]{2,1,0:T(8,128)S(1)}, u32[]{:S(2)}, u32[]{:S(2)}) collective-permute-start(f32[2,256,128]{2,1,0:T(8,128)S(1)} %get-tuple-element.38), channel_id=1, source_target_pairs={{0,2},{4,6},{8,10},{12,14},{2,0},{6,4},{10,8},{14,12},{1,3},{5,7},... | collective-permute-start | bytes 786440 | tf_op jit(solution)/shard_map/ppermute | solution.py:520
  2.9 14.8 %collective-permute-start.1 = (f32[2,256,128]{2,1,0:T(8,128)S(1)}, f32[2,256,128]{2,1,0:T(8,128)S(1)}, u32[]{:S(2)}, u32[]{:S(2)}) collective-permute-start(f32[2,256,128]{2,1,0:T(8,128)S(1)} %get-tuple-element.39), channel_id=1, source_target_pairs={{2,4},{6,8},{10,12},{4,2},{8,6},{12,10},{3,5},{7,9},{11,13},{5,3},... | collective-permute-start | bytes 786440 | tf_op jit(solution)/shard_map/ppermute | solution.py:520
  10.4 1.5 %collective-permute-start.2 = (f32[312,128]{1,0:T(8,128)S(1)}, f32[312,128]{1,0:T(8,128)S(1)}, u32[]{:S(2)}, u32[]{:S(2)}) collective-permute-start(f32[312,128]{1,0:T(8,128)S(1)} %get-tuple-element.40.own), channel_id=1, source_target_pairs={{0,1},{1,0},{2,3},{3,2},{4,5},{5,4},{6,7},{7,6},{8,9},{9,8},{10,11... | collective-permute-start | bytes 479240 | tf_op jit(solution)/shard_map/ppermute | solution.py:532
  12.0 21.9 %collective-permute-start.3 = (f32[2,208,128]{2,1,0:T(8,128)S(1)}, f32[2,208,128]{2,1,0:T(8,128)S(1)}, u32[]{:S(2)}, u32[]{:S(2)}) collective-permute-start(f32[2,208,128]{2,1,0:T(8,128)S(1)} %get-tuple-element.44), channel_id=1, source_target_pairs={{0,2},{4,6},{8,10},{12,14},{2,0},{6,4},{10,8},{14,12},{1,3},{5,7},... | collective-permute-start | bytes 638984 | tf_op jit(solution)/shard_map/ppermute | solution.py:520
  12.1 21.8 %collective-permute-start.4 = (f32[2,208,128]{2,1,0:T(8,128)S(1)}, f32[2,208,128]{2,1,0:T(8,128)S(1)}, u32[]{:S(2)}, u32[]{:S(2)}) collective-permute-start(f32[2,208,128]{2,1,0:T(8,128)S(1)} %get-tuple-element.45), channel_id=1, source_target_pairs={{2,4},{6,8},{10,12},{4,2},{8,6},{12,10},{3,5},{7,9},{11,13},{5,3},... | collective-permute-start | bytes 638984 | tf_op jit(solution)/shard_map/ppermute | solution.py:520
  17.8 27.5 %collective-permute-start.7 = (f32[2,320,128]{2,1,0:T(8,128)S(1)}, f32[2,320,128]{2,1,0:T(8,128)S(1)}, u32[]{:S(2)}, u32[]{:S(2)}) collective-permute-start(f32[2,320,128]{2,1,0:T(8,128)S(1)} %get-tuple-element.51), channel_id=1, source_target_pairs={{0,2},{4,6},{8,10},{12,14},{2,0},{6,4},{10,8},{14,12},{1,3},{5,7},... | collective-permute-start | bytes 983048 | tf_op jit(solution)/shard_map/ppermute | solution.py:520
  17.9 27.4 %collective-permute-start.8 = (f32[2,320,128]{2,1,0:T(8,128)S(1)}, f32[2,320,128]{2,1,0:T(8,128)S(1)}, u32[]{:S(2)}, u32[]{:S(2)}) collective-permute-start(f32[2,320,128]{2,1,0:T(8,128)S(1)} %get-tuple-element.53), channel_id=1, source_target_pairs={{2,4},{6,8},{10,12},{4,2},{8,6},{12,10},{3,5},{7,9},{11,13},{5,3},... | collective-permute-start | bytes 983048 | tf_op jit(solution)/shard_map/ppermute | solution.py:520
  38.6 12.2 %collective-permute-start.5 = (f32[2,240,128]{2,1,0:T(8,128)S(1)}, f32[2,240,128]{2,1,0:T(8,128)S(1)}, u32[]{:S(2)}, u32[]{:S(2)}) collective-permute-start(f32[2,240,128]{2,1,0:T(8,128)S(1)} %get-tuple-element.48), channel_id=1, source_target_pairs={{0,2},{4,6},{8,10},{12,14},{2,0},{6,4},{10,8},{14,12},{1,3},{5,7},... | collective-permute-start | bytes 737288 | tf_op jit(solution)/shard_map/ppermute | solution.py:520
  38.7 12.1 %collective-permute-start.6 = (f32[2,240,128]{2,1,0:T(8,128)S(1)}, f32[2,240,128]{2,1,0:T(8,128)S(1)}, u32[]{:S(2)}, u32[]{:S(2)}) collective-permute-start(f32[2,240,128]{2,1,0:T(8,128)S(1)} %get-tuple-element.49), channel_id=1, source_target_pairs={{2,4},{6,8},{10,12},{4,2},{8,6},{12,10},{3,5},{7,9},{11,13},{5,3},... | collective-permute-start | bytes 737288 | tf_op jit(solution)/shard_map/ppermute | solution.py:520
